TPU v7x, 32 devices: a whole 2x2x4 slice. The times are simulated.
32 devices in a mesh: section: 2 (over x), dp: 4 (over y, core), mp: 4 (over z).
Axes of the slice: x: 2, y: 2, z: 4, core: 2. Of those that a mesh axis runs over, the one named last changes fastest.
Arguments:
- tokens: bfloat16 [8, 768, 768], P('dp', 'mp'), may hold values from -6 to 6
- attn_gain: float32 [2, 768], P('section'), may hold values from 0.5 to 1.5
- w_query: bfloat16 [2, 768, 768], P('section', None, 'mp'), may hold values from -0.02734375 to 0.02734375
- w_key: bfloat16 [2, 768, 768], P('section', None, 'mp'), may hold values from -0.21875 to 0.21875
- w_value: bfloat16 [2, 768, 768], P('section', None, 'mp'), may hold values from -0.21875 to 0.21875
- w_out: bfloat16 [2, 768, 768], P('section', 'mp'), may hold values from -1.25 to 1.25
- ffn_gain: float32 [2, 768], P('section'), may hold values from 0.5 to 1.5
- w_gate: bfloat16 [2, 768, 2048], P('section', None, 'mp'), may hold values from -0.21875 to 0.21875
- w_up: bfloat16 [2, 768, 2048], P('section', None, 'mp'), may hold values from -0.21875 to 0.21875
- w_down: bfloat16 [2, 2048, 768], P('section', 'mp'), may hold values from -0.125 to 0.125
- rel_table: float32 [32, 12], P(None, 'mp'), may hold values from -4 to 4
- final_gain: float32 [768], replicated, may hold values from 0.5 to 1.5
- w_proj: bfloat16 [768, 128], replicated, may hold values from -0.21875 to 0.21875
- positives: int32 [64, 4], P('dp'), may hold values from -1 to 7, as said below
- retrieved: int32 [64, 32, 32], P('dp'), may hold values from 0 to 4095
Outputs:
- loss: float32 [], replicated
- d_inputs: bfloat16 [2, 8, 768, 768], P('section', 'dp', 'mp')
- grad_attn_gain: float32 [2, 768], P('section')
- grad_w_query: float32 [2, 768, 768], P('section', None, 'mp')
- grad_w_key: float32 [2, 768, 768], P('section', None, 'mp')
- grad_w_value: float32 [2, 768, 768], P('section', None, 'mp')
- grad_w_out: float32 [2, 768, 768], P('section', 'mp')
- grad_ffn_gain: float32 [2, 768], P('section')
- grad_w_gate: float32 [2, 768, 2048], P('section', None, 'mp')
- grad_w_up: float32 [2, 768, 2048], P('section', None, 'mp')
- grad_w_down: float32 [2, 2048, 768], P('section', 'mp')
- grad_rel_table: float32 [32, 12], P(None, 'mp')
- grad_final_gain: float32 [768], replicated
- grad_w_proj: float32 [768, 128], P(None, 'mp')
Inputs may be any that keep to these rules, and one draw needn't show every extreme that they name: `positives`: each row lists 1 to 4 different document numbers first and -1 in its remaining slots; some row lists 4, some row one.
All inputs are finite; a program needn't handle non-finite values.
Results may differ from a plain program's by a relative error of at most 0.035.
Values may be sent and summed in bfloat16 or wider, within the bound.
No kernel may reach another device: no remote copies, remote signals or barrier semaphores. Data moves between devices by JAX's collectives and lax.ppermute only.
A program may use at most 192 MiB of HBM per device.

v0:
```python
import functools

import jax
import jax.numpy as jnp
from jax import lax
from jax.experimental import pallas as pl
from jax.experimental.pallas import tpu as pltpu
from jax.sharding import PartitionSpec as P

D = 768
HEAD_DIM = 64
FF = 2048
PROJ = 128
DOC_LEN = 512
QRY_LEN = 32
QRYS_MB = 8
QRY_ROWS = QRYS_MB * QRY_LEN
MP = 4
QUARTER = D // MP
FQ = FF // MP
HEADS_Q = QUARTER // HEAD_DIM
BLK = 128
NBLK = DOC_LEN // BLK
QKV = 3 * QUARTER
SMALL = 16
F_HALF = 3 * FQ // 2

bucket_edges = (8, 12, 16, 23, 32, 46, 64, 91)
norm_eps = 1e-06
logit_scale = 16.0
highest = lax.Precision.HIGHEST
f32 = jnp.float32
bf16 = jnp.bfloat16

ACT, IS_DOC, ZPOS, RPOS = range(4)
VMEM_LIMIT = 56 * 1024 * 1024


def mm(a, b):
    return jnp.dot(a, b, preferred_element_type=f32)


def mm_t(a, b):
    return lax.dot_general(a, b, (((1,), (1,)), ((), ())), preferred_element_type=f32)


def t_mm(a, b):
    return lax.dot_general(a, b, (((0,), (0,)), ((), ())), preferred_element_type=f32)


def bucket_of(offset, half_count):
    spread = jnp.abs(offset)
    far_bucket = 7 + sum((spread >= edge).astype(jnp.int32) for edge in bucket_edges)
    near_bucket = jnp.where(spread < 8, spread, far_bucket)
    return near_bucket + half_count * (offset > 0).astype(jnp.int32)


class Copies:
    def __init__(self, sem, first=0):
        self.sem = sem
        self.next = first

    def __call__(self, source, target):
        copy = pltpu.make_async_copy(source, target, self.sem.at[self.next])
        self.next += 1
        copy.start()
        return copy


def get_rows(copy, halves, target, doc):
    count = 2 if doc else 1
    return [copy(halves[i], target.at[pl.ds(i * QRY_ROWS, QRY_ROWS)]) for i in range(count)]


def put_rows(copy, source, halves, doc):
    count = 2 if doc else 1
    return [copy(source.at[pl.ds(i * QRY_ROWS, QRY_ROWS)], halves[i]) for i in range(count)]


def wait_all(copies):
    for copy in copies:
        copy.wait()


class Weights:
    def __init__(self, flags, chunk, target, sem, lanes=None):
        self.z, self.r = flags[ZPOS], flags[RPOS]
        self.own, self.pieces = chunk[0], chunk[1:]
        self.target, self.sem = target, sem
        self.lanes = pl.ds(0, target.shape[2]) if lanes is None else lanes

    def copies(self, s):
        if s == 0:
            return [pltpu.make_async_copy(self.own, self.target.at[self.z, :, self.lanes], self.sem.at[0, 0])]
        return [
            pltpu.make_async_copy(
                self.pieces[4 * (s - 1) + k],
                self.target.at[self.z ^ s, rows_at(self.r ^ bits, QUARTER), self.lanes],
                self.sem.at[s, k],
            )
            for k, bits in enumerate((0, 2, 1, 3))
        ]

    def start(self):
        for s in range(MP):
            start_all(self.copies(s))

    def each(self, s, act):
        for k in range(MP):
            pl.when(s == k)(lambda k=k: act(self.copies(k)))

    def start_slot(self, s):
        self.each(s, start_all)

    def wait_slot(self, s):
        self.each(s, wait_all)


N_CHUNK = 13


def start_all(copies):
    for copy in copies:
        copy.start()


def rows_at(index, size):
    return pl.ds(pl.multiple_of(index * size, size), size)


def offset_bias(table):
    column = lax.broadcasted_iota(jnp.int32, (table.shape[0], 4 * BLK), 1)
    bucket = lax.broadcasted_iota(jnp.int32, (table.shape[0], 4 * BLK), 0)
    offset = jnp.where(column < 2 * BLK, -column, 4 * BLK - column)
    hot = (bucket_of(offset, table.shape[0] // 2) == bucket).astype(f32)
    return lax.dot_general(table, hot, (((0,), (0,)), ((), ())), precision=highest, preferred_element_type=f32)


def near_blocks(offsets_ref, head):
    row = jnp.broadcast_to(offsets_ref[pl.ds(head, 1), :], (BLK, 4 * BLK))
    rolled = pltpu.roll(row, 0, 1, stride=1, stride_axis=0)
    return {0: rolled[:, :BLK], -1: rolled[:, BLK : 2 * BLK], 1: rolled[:, 3 * BLK :]}


def bias_matrix(offsets_ref, table_ref, head):
    far_up = jnp.full((BLK, BLK), table_ref[31, head], f32)
    far_low = jnp.full((BLK, BLK), table_ref[15, head], f32)
    near = near_blocks(offsets_ref, head)

    def block(bj, bi):
        if bj - bi in near:
            return near[bj - bi]
        return far_up if bj > bi else far_low

    return jnp.concatenate(
        [jnp.concatenate([block(bj, bi) for bi in range(NBLK)], axis=1) for bj in range(NBLK)], axis=0
    )


def query_bias(offsets_ref, head):
    j = lax.broadcasted_iota(jnp.int32, (BLK, BLK), 0) // QRY_LEN
    i = lax.broadcasted_iota(jnp.int32, (BLK, BLK), 1) // QRY_LEN
    return jnp.where(i == j, near_blocks(offsets_ref, head)[0], -1e30)


def rms_parts(values):
    return lax.rsqrt(jnp.mean(values * values, axis=-1, keepdims=True) + norm_eps)


def rms_back(values, gain, grad):
    scale = rms_parts(values)
    weighted = grad * gain
    inner = jnp.mean(values * weighted, axis=-1, keepdims=True)
    out = scale * (weighted - values * (scale * scale * inner))
    gain_grad = jnp.sum(grad * values * scale, axis=0, keepdims=True)
    return out, gain_grad


def by_kind(flags, body):
    pl.when(flags[IS_DOC] == 1)(lambda: body(DOC_LEN, True))
    pl.when(flags[IS_DOC] == 0)(lambda: body(QRY_ROWS, False))


def head_slices(hh):
    at = hh * HEAD_DIM
    return (
        slice(at, at + HEAD_DIM),
        slice(QUARTER + at, QUARTER + at + HEAD_DIM),
        slice(2 * QUARTER + at, 2 * QUARTER + at + HEAD_DIM),
        slice(at, at + HEAD_DIM),
    )


def attn_fwd_kernel(flags, table, table_ref, attn_gain_ref, ffn_gain_ref, x_low, x_high, *refs):
    weights, refs = refs[:N_CHUNK], refs[N_CHUNK:]
    normed_out, qkv_out, lse_out, mixed_out, middle_out, normed_ffn_out = refs[:6]
    x_ref, offsets_ref, normed_ref, qkv_ref, lse_ref, mixed_ref, middle_ref, normed_ffn_ref = refs[6:14]
    wa, sem, asem, zsem = refs[14:]
    weights = Weights(flags, weights, wa, asem)
    def one_head(z, hh, rows, bias):
        qs, ks, vs, ms = head_slices(hh)
        q, k, v = qkv_ref[z, rows, qs], qkv_ref[z, rows, ks], qkv_ref[z, rows, vs]
        scores = mm_t(k, q) + bias
        peak = jnp.max(scores, axis=0, keepdims=True)
        weights = jnp.exp(scores - peak)
        total = jnp.sum(weights, axis=0, keepdims=True)
        mixed = t_mm(v, weights.astype(bf16)) * (1.0 / total)
        lse_ref[z, hh : hh + 1, rows] = peak + jnp.log(total)
        mixed_ref[z, rows, ms] = mixed.T.astype(bf16)

    def body(rows, doc):
        put = Copies(sem)
        outs = []
        get_x = get_rows(put, (x_low, x_high), x_ref, doc)
        weights.start()
        offsets_ref[...] = offset_bias(table_ref[...])
        wait_all(get_x)

        def send(source, target):
            outs.append(put(source.at[pl.ds(0, rows)], target.at[pl.ds(0, rows)]))

        def parts(z):
            return [
                pltpu.make_async_copy(a.at[z, pl.ds(0, rows)], b.at[z, pl.ds(0, rows)], zsem.at[z, i])
                for i, (a, b) in enumerate(((qkv_ref, qkv_out), (mixed_ref, mixed_out)))
            ]

        x = x_ref[:rows].astype(f32)
        normed_ref[:rows] = (x * rms_parts(x) * attn_gain_ref[...]).astype(bf16)
        send(normed_ref, normed_out)

        @pl.loop(0, MP)
        def _(s):
            z = flags[ZPOS] ^ s
            weights.wait_slot(s)
            qkv_ref[z, :rows] = mm_t(normed_ref[:rows], wa[z, :QKV]).astype(bf16)
            for hh in range(HEADS_Q):
                head = z * HEADS_Q + hh
                if doc:
                    one_head(z, hh, slice(0, DOC_LEN), bias_matrix(offsets_ref, table, head))
                else:
                    bias = query_bias(offsets_ref, head)
                    for b in range(QRY_ROWS // BLK):
                        one_head(z, hh, slice(b * BLK, (b + 1) * BLK), bias)
            start_all(parts(z))

        outs.append(put(lse_ref, lse_out))
        middle_ref[:rows] = x_ref[:rows].astype(f32)

        @pl.loop(0, MP)
        def _(z):
            middle_ref[:rows] += mm(mixed_ref[z, :rows], wa[z, QKV:])

        middle = middle_ref[:rows]
        send(middle_ref, middle_out)
        normed_ffn_ref[:rows] = (middle * rms_parts(middle) * ffn_gain_ref[...]).astype(bf16)
        send(normed_ffn_ref, normed_ffn_out)

        @pl.loop(0, MP)
        def _(z):
            wait_all(parts(z))

        wait_all(outs)

    @pl.when(flags[ACT] == 1)
    def _():
        by_kind(flags, body)


def ffn_fwd_kernel(flags, final_gain_ref, proj_ref, middle_hbm, normed_hbm, *refs):
    first, second, refs = refs[:N_CHUNK], refs[N_CHUNK : 2 * N_CHUNK], refs[2 * N_CHUNK :]
    out_out, low_low, low_high, hidden_out, ga_out, gb_out, final_out, embed_out = refs[:8]
    normed_ref, out_ref, low_ref, hidden_ref, ga_ref, gb_ref, final_ref, embed_ref = refs[8:16]
    wf, sem, fsem, gsem, zsem = refs[16:]
    first = Weights(flags, first, wf, fsem, pl.ds(0, F_HALF))
    second = Weights(flags, second, wf, gsem, pl.ds(F_HALF, F_HALF))

    def body(rows, doc):
        copy = Copies(sem)
        get_normed = copy(normed_hbm.at[pl.ds(0, rows)], normed_ref.at[pl.ds(0, rows)])
        get_middle = copy(middle_hbm.at[pl.ds(0, rows)], out_ref.at[pl.ds(0, rows)])
        first.start_slot(0)
        second.start_slot(0)

        def parts(z):
            pairs = ((hidden_ref, hidden_out), (ga_ref, ga_out), (gb_ref, gb_out))
            return [
                pltpu.make_async_copy(a.at[z, pl.ds(0, rows)], b.at[z, pl.ds(0, rows)], zsem.at[z, i])
                for i, (a, b) in enumerate(pairs)
            ]

        get_normed.wait()
        get_middle.wait()

        @pl.loop(0, MP)
        def _(s):
            z = flags[ZPOS] ^ s

            first.start_slot(s + 1)
            second.start_slot(s + 1)
            first.wait_slot(s)
            second.wait_slot(s)
            normed = normed_ref[:rows]
            gate = mm(normed, wf[z, :, :FQ])
            up = mm(normed, wf[z, :, FQ : 2 * FQ])
            coef = 0.7978845608028654
            square = gate * gate
            tanh = jnp.tanh(coef * gate * (1.0 + 0.044715 * square))
            half = 0.5 + 0.5 * tanh
            gelu = gate * half
            slope = half + (0.5 * coef) * gate * (1.0 - tanh * tanh) * (1.0 + 3 * 0.044715 * square)
            hidden = (gelu * up).astype(bf16)
            hidden_ref[z, :rows] = hidden
            ga_ref[z, :rows] = (up * slope).astype(bf16)
            gb_ref[z, :rows] = gelu.astype(bf16)
            start_all(parts(z))
            out_ref[:rows] += mm_t(hidden, wf[z, :, 2 * FQ :])

        low_ref[:rows] = out_ref[:rows].astype(bf16)
        if not doc:
            out_ref[rows:] = jnp.zeros((DOC_LEN - rows, D), f32)
            final_ref[rows:] = jnp.zeros((DOC_LEN - rows, D), bf16)
        outs = put_rows(copy, low_ref, (low_low, low_high), doc) + [copy(out_ref, out_out)]
        out = out_ref[:rows]
        final_ref[:rows] = (out * rms_parts(out) * final_gain_ref[...]).astype(bf16)
        embed_ref[:rows] = mm(final_ref[:rows], proj_ref[...]).astype(bf16)
        outs.append(copy(embed_ref.at[pl.ds(0, rows)], embed_out.at[pl.ds(0, rows)]))
        outs.append(copy(final_ref, final_out))

        @pl.loop(0, MP)
        def _(z):
            wait_all(parts(z))

        wait_all(outs)

    @pl.when(flags[ACT] == 1)
    def _():
        by_kind(flags, body)


def ffn_bwd_kernel(
    flags, gain_ref, gout_low, gout_high, middle_hbm, normed_hbm, hidden_hbm, ga_hbm, gb_hbm,
    *refs,
):
    gmid_out, dgain_out, *df_outs = refs[-24:-18]
    gout_ref, middle_ref, normed_ref, hidden_ref, ga_ref, gb_ref, gmid_ref, dgain_ref = refs[-18:-10]
    wf, gout_t, normed_t, df_buf, gn, sem, fsem, gsem, ksem, osem = refs[-10:]
    first = Weights(flags, refs[:N_CHUNK], wf, fsem, pl.ds(0, F_HALF))
    second = Weights(flags, refs[N_CHUNK : 2 * N_CHUNK], wf, gsem, pl.ds(F_HALF, F_HALF))

    def outs(s, core):
        slot, half, z = s % 2, D // 2, flags[ZPOS] ^ s
        copies = []
        for i, out in enumerate(df_outs):
            rows = pl.ds((core if i % 2 == 0 else 1 - core) * half, half)
            lanes = pl.ds(i // 2 * F_HALF, F_HALF)
            copies.append(pltpu.make_async_copy(df_buf.at[slot, rows, lanes], out.at[z], osem.at[slot, i]))
        return copies

    def body(rows, doc):
        core = 0 if doc else 1
        copy = Copies(sem)

        def get(source, target):
            return copy(source.at[pl.ds(0, rows)], target.at[pl.ds(0, rows)])

        get_gout = get_rows(copy, (gout_low, gout_high), gout_ref, doc)
        get_normed = get(normed_hbm, normed_ref)
        kept = ((ga_hbm, ga_ref), (gb_hbm, gb_ref), (hidden_hbm, hidden_ref))

        def part(z):
            return [
                pltpu.make_async_copy(a.at[z, pl.ds(0, rows)], b.at[z, pl.ds(0, rows)], ksem.at[z, i])
                for i, (a, b) in enumerate(kept)
            ]

        first.start_slot(0)
        second.start_slot(0)
        start_all(part(flags[ZPOS]))
        get_middle = get(middle_hbm, middle_ref)
        wait_all(get_gout)
        gout_t[:, :rows] = gout_ref[:rows].T
        get_normed.wait()
        normed_t[:, :rows] = normed_ref[:rows].T
        gn[:rows] = jnp.zeros((rows, D), f32)

        @pl.loop(0, MP)
        def _(s):
            z = flags[ZPOS] ^ s
            pl.when(s >= 2)(lambda: wait_all(outs(s - 2, core)))

            first.start_slot(s + 1)
            second.start_slot(s + 1)
            pl.when(s + 1 < MP)(lambda: start_all(part(flags[ZPOS] ^ (s + 1))))
            first.wait_slot(s)
            second.wait_slot(s)
            wait_all(part(z))
            slot = s % 2
            grad_hidden = mm(gout_ref[:rows], wf[z, :, 2 * FQ :])
            grad_gate = (grad_hidden * ga_ref[z, :rows].astype(f32)).astype(bf16)
            grad_up = (grad_hidden * gb_ref[z, :rows].astype(f32)).astype(bf16)
            df_buf[slot, :, :FQ] = mm(normed_t[:, :rows], grad_gate).astype(bf16)
            df_buf[slot, :, FQ : 2 * FQ] = mm(normed_t[:, :rows], grad_up).astype(bf16)
            df_buf[slot, :, 2 * FQ :] = mm(gout_t[:, :rows], hidden_ref[z, :rows]).astype(bf16)
            start_all(outs(s, core))
            gn[:rows] += mm_t(grad_gate, wf[z, :, :FQ]) + mm_t(grad_up, wf[z, :, FQ : 2 * FQ])

        get_middle.wait()
        back, gain_grad = rms_back(middle_ref[:rows], gain_ref[...], gn[:rows])
        gmid_ref[:rows] = gout_ref[:rows].astype(f32) + back
        dgain_ref[...] = gain_grad
        last = [copy(gmid_ref.at[pl.ds(0, rows)], gmid_out.at[pl.ds(0, rows)]), copy(dgain_ref, dgain_out)]
        for s in (MP - 2, MP - 1):
            wait_all(outs(s, core))
        wait_all(last)

    @pl.when(flags[ACT] == 1)
    def _():
        by_kind(flags, body)


def attn_bwd_kernel(
    flags, table, table_ref, gain_ref, band_ref, ffn_gain_ref, early_ref, gmid_hbm, x_low, x_high, normed_hbm, qkv_hbm, lse_hbm,
    mixed_hbm, *refs,
):
    gx_low, gx_high, dgain_out, *da_outs = refs[-27:-22]
    gmid_ref, x_ref, offsets_ref, normed_ref, qkv_ref, lse_ref, mixed_ref, gx_ref, dgain_ref, diag_ref = refs[-22:-12]
    wa, gmb, gmix, gqkv, da_buf, gn, rows_buf, sem, asem, ksem, osem, rsem = refs[-12:]
    weights = Weights(flags, refs[:N_CHUNK], wa, asem)

    def one_head(z, hh, rows, bias):
        qs, ks, vs, ms = head_slices(hh)
        q, k, v = qkv_ref[z, rows, qs], qkv_ref[z, rows, ks], qkv_ref[z, rows, vs]
        go = gmix[rows, ms]
        out = mixed_ref[z, rows, ms].astype(f32)
        delta = jnp.sum((go.astype(f32) * out).T, axis=0, keepdims=True)
        probs = jnp.exp(mm_t(k, q) + bias - lse_ref[z, hh : hh + 1, rows])
        grad_scores = probs * (mm_t(v, go) - delta)
        low = grad_scores.astype(bf16)
        gqkv[rows, qs] = t_mm(k, low).T.astype(bf16)
        gqkv[rows, ks] = mm(low, q).astype(bf16)
        gqkv[rows, vs] = mm(probs.astype(bf16), go).astype(bf16)
        return grad_scores

    def band_sums(up, mid, low):
        blank = jnp.zeros((BLK, BLK), f32)
        band = jnp.concatenate([up, mid, low, blank], axis=1)
        width = 4 * BLK

        def left(part, by):
            return pltpu.roll(part, width - by, 1) if by else part

        eight = functools.reduce(jnp.add, [left(band[g : g + 8], g) for g in range(0, BLK, 8)])
        return functools.reduce(jnp.add, [left(eight[r : r + 1], r) for r in range(8)])

    def outs(s, core):
        slot, z = s % 2, flags[ZPOS] ^ s
        copies = []
        for i, out in enumerate(da_outs):
            for half in range(2):
                rows = pl.ds((core if i == 0 else 1 - core) * (D // 2) + half * QUARTER, QUARTER)
                target = out.at[z, half, pl.ds(0, QUARTER), :]
                copies.append(pltpu.make_async_copy(da_buf.at[slot, rows, :], target, osem.at[slot, 2 * i + half]))
        return copies

    def body(rows, doc):
        core = 0 if doc else 1
        copy = Copies(sem)

        def get(source, target):
            return copy(source.at[pl.ds(0, rows)], target.at[pl.ds(0, rows)])

        get_gmid = get(gmid_hbm, gmid_ref)
        get_lse = copy(lse_hbm, lse_ref)
        kept = ((qkv_hbm, qkv_ref), (mixed_hbm, mixed_ref))

        def part(z):
            return [
                pltpu.make_async_copy(a.at[z, pl.ds(0, rows)], b.at[z, pl.ds(0, rows)], ksem.at[z, i])
                for i, (a, b) in enumerate(kept)
            ]

        weights.start_slot(0)
        start_all(part(flags[ZPOS]))
        offsets_ref[...] = offset_bias(table_ref[...])
        get_normed = get(normed_hbm, normed_ref)
        get_x = get_rows(copy, (x_low, x_high), x_ref, doc)
        get_gmid.wait()
        gmb[:rows] = gmid_ref[:rows].astype(bf16)
        gn[:rows] = jnp.zeros((rows, D), f32)
        get_lse.wait()
        get_normed.wait()

        @pl.loop(0, MP)
        def _(s):
            z = flags[ZPOS] ^ s
            pl.when(s >= 2)(lambda: wait_all(outs(s - 2, core)))

            weights.start_slot(s + 1)
            pl.when(s + 1 < MP)(lambda: start_all(part(flags[ZPOS] ^ (s + 1))))
            weights.wait_slot(s)
            wait_all(part(z))
            slot = s % 2
            gmix[:rows] = mm_t(gmb[:rows], wa[z, QKV:]).astype(bf16)
            for hh in range(HEADS_Q):
                head = z * HEADS_Q + hh
                if doc:
                    grads = one_head(z, hh, slice(0, DOC_LEN), bias_matrix(offsets_ref, table, head))

                    def blocks(test):
                        picked = [
                            grads[bj * BLK : (bj + 1) * BLK, bi * BLK : (bi + 1) * BLK]
                            for bj in range(NBLK)
                            for bi in range(NBLK)
                            if test(bj - bi)
                        ]
                        return functools.reduce(jnp.add, picked)

                    sums = band_sums(blocks(lambda d: d == 1), blocks(lambda d: d == 0), blocks(lambda d: d == -1))
                    far_up = jnp.sum(blocks(lambda d: d > 1), axis=0, keepdims=True)
                    far_low = jnp.sum(blocks(lambda d: d < -1), axis=0, keepdims=True)
                    diag_ref[z, hh : hh + 1, :] = jnp.concatenate([sums, far_up, far_low], axis=1)
                else:
                    grads = jnp.zeros((BLK, BLK), f32)
                    bias = query_bias(offsets_ref, head)
                    for b in range(QRY_ROWS // BLK):
                        grads = grads + one_head(z, hh, slice(b * BLK, (b + 1) * BLK), bias)
                    blank = jnp.zeros((BLK, BLK), f32)
                    sums = band_sums(blank, grads, blank)
                    diag_ref[z, hh : hh + 1, :] = jnp.concatenate([sums, jnp.zeros((1, 2 * BLK), f32)], axis=1)
            grads = gqkv[:rows]
            da_buf[slot, :QKV] = t_mm(grads, normed_ref[:rows]).astype(bf16)
            da_buf[slot, QKV:] = t_mm(mixed_ref[z, :rows], gmb[:rows]).astype(bf16)
            start_all(outs(s, core))
            gn[:rows] += mm(grads, wa[z, :QKV])

        wait_all(get_x)
        back, gain_grad = rms_back(x_ref[:rows].astype(f32), gain_ref[...], gn[:rows])
        gx_ref[:rows] = (gmid_ref[:rows] + back).astype(bf16)
        dgain_ref[...] = gain_grad
        last = put_rows(copy, gx_ref, (gx_low, gx_high), doc) + [copy(dgain_ref, dgain_out)]
        for z in range(MP):
            sums = jnp.dot(diag_ref[z], band_ref[...], precision=highest, preferred_element_type=f32)
            shared = [
                jnp.concatenate([sums[:HEADS_Q], jnp.zeros((HEADS_Q, D - BLK), f32)], axis=1),
                gain_grad,
                ffn_gain_ref[...],
                early_ref[PROJ : PROJ + 3],
            ]
            shared = jnp.concatenate(shared, axis=0)
            for which, side in enumerate((core, 1 - core)):
                for half in range(2):
                    first = z * (PROJ // MP) + side * 16 + half * 8
                    both = jnp.concatenate([shared, early_ref[first : first + 8]], axis=0)
                    rows_buf[which, z, half] = both.astype(bf16)
        for which, out in enumerate(da_outs):
            target = out.at[:, :, pl.ds(QUARTER, SMALL), :]
            last.append(pltpu.make_async_copy(rows_buf.at[which], target, rsem.at[which]))
            last[-1].start()
        for s in (MP - 2, MP - 1):
            wait_all(outs(s, core))
        wait_all(last)

    @pl.when(flags[ACT] == 1)
    def _():
        by_kind(flags, body)


def put_all(refs):
    count = len(refs) // 2
    copies = [pltpu.make_async_copy(refs[count + i], refs[i], refs[-1].at[i]) for i in range(count)]
    start_all(copies)
    wait_all(copies)


def finish_ffn_kernel(flags, mine1, other1, mine2, other2, *refs):
    gate_ref, up_ref, down_ref = refs[3:6]
    core = flags[RPOS] % 2
    half = D // 2
    for side, first, second in ((core, mine1, mine2), (1 - core, other1, other2)):
        rows = rows_at(side, half)
        low = first[...].reshape(half, F_HALF).astype(f32)
        high = second[...].reshape(half, F_HALF).astype(f32)
        gate_ref[rows, :] = low[:, :FQ]
        up_ref[rows, : F_HALF - FQ] = low[:, FQ:]
        up_ref[rows, F_HALF - FQ :] = high[:, : 2 * FQ - F_HALF]
        down = high[:, 2 * FQ - F_HALF :].T

        @pl.when(side == 0)
        def _():
            down_ref[:, :half] = down

        @pl.when(side == 1)
        def _():
            down_ref[:, half:] = down

    put_all(refs)


def finish_attn_kernel(flags, mine, other, *refs):
    buffers = refs[4:8]
    core = flags[RPOS] % 2
    for side in range(2):

        @pl.when(core == side)
        def _():
            for i in range(2):
                buffers[2 * side + i][...] = mine[i, :QUARTER].astype(f32)
                buffers[2 - 2 * side + i][...] = other[i, :QUARTER].astype(f32)

    put_all(refs)


def vmem():
    return pl.BlockSpec(memory_space=pltpu.VMEM)


def smem():
    return pl.BlockSpec(memory_space=pltpu.SMEM)


def hbm():
    return pl.BlockSpec(memory_space=pl.ANY)


def shape(dims, kind):
    return jax.ShapeDtypeStruct(dims, kind)


def params():
    return pltpu.CompilerParams(vmem_limit_bytes=VMEM_LIMIT)


def cost(microseconds):
    return pl.CostEstimate(flops=int(microseconds * 1e9), bytes_accessed=16 * 1024 * 1024, transcendentals=0)


def count_kernel(flags, hits_ref, counts_out, buffer, sem):
    width = buffer.shape[2]
    blocks = hits_ref.shape[1] // width

    def put(i):
        lanes = pl.ds(pl.multiple_of(i * width, width), width)
        return pltpu.make_async_copy(buffer.at[i % 2], counts_out.at[:, lanes], sem.at[i % 2])

    @pl.when(jnp.logical_and(flags[ACT] == 1, flags[IS_DOC] == 1))
    def _():
        @pl.loop(0, blocks)
        def _(i):
            pl.when(i >= 2)(lambda: put(i - 2).wait())
            hits = hits_ref[:, pl.ds(pl.multiple_of(i * width, width), width)]
            for row in range(0, DOC_LEN, BLK):
                places = lax.broadcasted_iota(jnp.int32, (BLK, width), 0) + row
                total = jnp.zeros((BLK, width), f32)
                for k in range(hits.shape[0]):
                    total = total + (hits[k : k + 1] == places).astype(f32)
                buffer[i % 2, row : row + BLK] = total.astype(bf16)
            put(i).start()

        put(blocks - 2).wait()
        put(blocks - 1).wait()


def count_hits(flags, hits):
    width = BLK
    return pl.pallas_call(
        count_kernel,
        in_specs=[smem(), vmem()],
        out_specs=hbm(),
        out_shape=shape((DOC_LEN, hits.shape[1]), bf16),
        scratch_shapes=[pltpu.VMEM((2, DOC_LEN, width), bf16), pltpu.SemaphoreType.DMA((2,))],
        compiler_params=params(),
        cost_estimate=cost(8),
        name="count_hits",
    )(flags, hits)


QUARTERS = (MP, DOC_LEN, FQ)
ROWS = (DOC_LEN, D)
HALF_ROWS = (QRY_ROWS, D)


def on_vmem(shapes):
    return [pltpu.VMEM(s.shape, s.dtype) for s in shapes]


def attn_fwd(flags, table, x, attn_gain, ffn_gain, attn_weights):
    results = [
        shape(ROWS, bf16),
        shape((MP, DOC_LEN, QKV), bf16),
        shape((MP, 8, DOC_LEN), f32),
        shape((MP, DOC_LEN, QUARTER), bf16),
        shape(ROWS, f32),
        shape(ROWS, bf16),
    ]
    return pl.pallas_call(
        attn_fwd_kernel,
        in_specs=[smem()] * 2 + [vmem()] * 3 + [hbm()] * (2 + N_CHUNK),
        out_specs=[hbm()] * 6,
        out_shape=results,
        scratch_shapes=on_vmem([shape(ROWS, bf16), shape((table.shape[1], 4 * BLK), f32)] + results)
        + [
            pltpu.VMEM((MP, D, D), bf16),
            pltpu.SemaphoreType.DMA((10,)),
            pltpu.SemaphoreType.DMA((MP, 4)),
            pltpu.SemaphoreType.DMA((MP, 2)),
        ],
        compiler_params=params(),
        cost_estimate=cost(14),
        name="attn_fwd",
    )(flags, table, table, attn_gain, ffn_gain, *x, *attn_weights)


def ffn_fwd(flags, final_gain, w_proj, middle, normed, ffn_weights):
    buffers = [shape(ROWS, f32), shape(ROWS, bf16)] + [shape(QUARTERS, bf16)] * 3
    buffers += [shape(ROWS, bf16), shape((DOC_LEN, PROJ), bf16)]
    results = buffers[:1] + [shape(HALF_ROWS, bf16)] * 2 + buffers[2:]
    return pl.pallas_call(
        ffn_fwd_kernel,
        in_specs=[smem()] + [vmem()] * 2 + [hbm()] * (2 + 2 * N_CHUNK),
        out_specs=[hbm()] * 8,
        out_shape=results,
        scratch_shapes=on_vmem([shape(ROWS, bf16)] + buffers)
        + [
            pltpu.VMEM((MP, D, 3 * FQ), bf16),
            pltpu.SemaphoreType.DMA((8,)),
            pltpu.SemaphoreType.DMA((MP, 4)),
            pltpu.SemaphoreType.DMA((MP, 4)),
            pltpu.SemaphoreType.DMA((MP, 3)),
        ],
        compiler_params=params(),
        cost_estimate=cost(10),
        name="ffn_fwd",
    )(flags, final_gain, w_proj, middle, normed, *ffn_weights)


def score_kernel(flags, query_ref, embed_ref, counts_ref, shares_ref, share_query_ref, mass_ref):
    @pl.when(jnp.logical_and(flags[ACT] == 1, flags[IS_DOC] == 1))
    def _():
        sims = mm_t(embed_ref[...], query_ref[...])
        weighted = jnp.exp(sims * PROJ ** (-0.5)) * counts_ref[...].astype(f32)
        mass = jnp.sum(weighted, axis=0, keepdims=True)
        mass_ref[...] = mass
        shares = (weighted * (1.0 / (1.0 + mass))).astype(bf16)
        shares_ref[...] = shares
        share_query_ref[...] = t_mm(shares, embed_ref[...])


def score(flags, query_slots, embed, counts):
    tokens = query_slots.shape[0]
    width = DOC_LEN
    return pl.pallas_call(
        score_kernel,
        grid=(tokens // width,),
        in_specs=[
            smem(),
            pl.BlockSpec((width, PROJ), lambda i: (i, 0)),
            pl.BlockSpec((DOC_LEN, PROJ), lambda i: (0, 0)),
            pl.BlockSpec((DOC_LEN, width), lambda i: (0, i)),
        ],
        out_specs=[
            pl.BlockSpec((DOC_LEN, width), lambda i: (0, i)),
            pl.BlockSpec((width, PROJ), lambda i: (i, 0)),
            pl.BlockSpec((1, width), lambda i: (0, i)),
        ],
        out_shape=[shape((DOC_LEN, tokens), bf16), shape((tokens, PROJ), f32), shape((1, tokens), f32)],
        compiler_params=params(),
        cost_estimate=cost(4),
        name="score",
    )(flags, query_slots, embed, counts)


def coef_kernel(flags, logits_ref, chosen_ref, expand_ref, share_ref, coef_ref, grad_ref, loss_ref):
    @pl.when(jnp.logical_and(flags[ACT] == 1, flags[IS_DOC] == 1))
    def _():
        logits = logits_ref[...]
        n_queries = logits.shape[1]
        spread = jnp.exp(logits - jnp.max(logits, axis=0, keepdims=True))
        all_total = jnp.sum(spread, axis=0, keepdims=True)
        pos_total = jnp.sum(chosen_ref[...] * spread, axis=0, keepdims=True)
        own = spread[0:1]
        grad = own / all_total - chosen_ref[0:1] * own / pos_total
        loss = jnp.sum(jnp.log(all_total) - jnp.log(pos_total), axis=1, keepdims=True) / n_queries
        loss_ref[...] = jnp.broadcast_to(loss, loss_ref.shape)
        grad = jnp.broadcast_to(grad * (logit_scale / QRY_LEN * PROJ ** (-0.5) / n_queries), (8, n_queries))
        coef = jnp.dot(grad, expand_ref[...], precision=highest, preferred_element_type=f32)
        coef_ref[...] = coef[0:1]
        grad_ref[...] = (share_ref[...] * coef.T[:, 0:1]).astype(bf16)


def coefs(flags, logits, chosen, expand, share_query):
    return pl.pallas_call(
        coef_kernel,
        in_specs=[smem()] + [vmem()] * 4,
        out_specs=[vmem()] * 3,
        out_shape=[
            shape((1, share_query.shape[0]), f32),
            shape(share_query.shape, bf16),
            shape((1, BLK), f32),
        ],
        compiler_params=params(),
        cost_estimate=cost(3),
        name="coefs",
    )(flags, logits, chosen, expand, share_query)


def head_bwd_kernel(
    flags, shares_ref, query_ref, coef_ref, grad_query_ref, loss_ref, normed_ref, out_ref, gain_ref, proj_ref,
    gout_low, gout_high, early_ref, grad_embed,
):
    @pl.when(jnp.logical_and(flags[ACT] == 1, flags[IS_DOC] == 1))
    def _():
        scaled = (shares_ref[...].astype(f32) * coef_ref[...]).astype(bf16)
        grad_embed[...] = mm(scaled, query_ref[...]).astype(bf16)

    @pl.when(flags[IS_DOC] == 0)
    def _():
        grad_embed[:QRY_ROWS] = grad_query_ref[...]
        grad_embed[QRY_ROWS:] = jnp.zeros((DOC_LEN - QRY_ROWS, PROJ), bf16)

    @pl.when(flags[ACT] == 1)
    def _():
        back, gain_grad = rms_back(out_ref[...], gain_ref[...], mm_t(grad_embed[...], proj_ref[...]))
        back = back.astype(bf16)
        gout_low[...] = back[:QRY_ROWS]
        gout_high[...] = back[QRY_ROWS:]
        early_ref[:PROJ] = t_mm(grad_embed[...], normed_ref[...]).astype(bf16)
        loss = jnp.concatenate([loss_ref[...]] * (D // BLK), axis=1)
        high = loss.astype(bf16).astype(f32)
        rest = jnp.zeros((13, D), f32)
        early_ref[PROJ:] = jnp.concatenate([gain_grad, high, loss - high, rest], axis=0).astype(bf16)

    @pl.when(flags[ACT] == 0)
    def _():
        early_ref[...] = jnp.zeros_like(early_ref)


def head_bwd(flags, shares, query_slots, coef, grad_query, loss, normed, out, gain, proj):
    return pl.pallas_call(
        head_bwd_kernel,
        in_specs=[smem()] + [vmem()] * 9,
        out_specs=[vmem()] * 3,
        out_shape=[shape(HALF_ROWS, bf16)] * 2 + [shape((PROJ + 16, D), bf16)],
        scratch_shapes=[pltpu.VMEM((DOC_LEN, PROJ), bf16)],
        compiler_params=params(),
        cost_estimate=cost(5),
        name="head_bwd",
    )(flags, shares, query_slots, coef, grad_query, loss, normed, out, gain, proj)


def finish(kernel, flags, results, *values):
    return pl.pallas_call(
        kernel,
        in_specs=[smem()] + [vmem()] * len(values),
        out_specs=[pl.BlockSpec(memory_space=pltpu.HBM)] * len(results),
        out_shape=[pltpu.HBM(r, f32) for r in results],
        scratch_shapes=on_vmem([shape(r, f32) for r in results]) + [pltpu.SemaphoreType.DMA((len(results),))],
        compiler_params=params(),
        cost_estimate=cost(3),
        name="finish",
    )(flags, *values)


def ffn_bwd(flags, gout, middle, gain, normed, hidden, ga, gb, ffn_weights, prev):
    results = [shape(ROWS, f32), shape((1, D), f32)]
    results += [shape((MP, D // 2, F_HALF), bf16)] * 4
    prev = prev or []
    return pl.pallas_call(
        ffn_bwd_kernel,
        in_specs=[smem(), vmem()] + [hbm()] * (7 + 2 * N_CHUNK + len(prev)),
        out_specs=[hbm()] * 6,
        out_shape=results,
        input_output_aliases={9 + 2 * N_CHUNK + i: 1 + i for i in range(len(prev))},
        scratch_shapes=on_vmem([shape(ROWS, bf16), shape(ROWS, f32), shape(ROWS, bf16)] + [shape(QUARTERS, bf16)] * 3)
        + on_vmem(results[:2])
        + [
            pltpu.VMEM((MP, D, 3 * FQ), bf16),
            pltpu.VMEM((D, DOC_LEN), bf16),
            pltpu.VMEM((D, DOC_LEN), bf16),
            pltpu.VMEM((2, D, 3 * FQ), bf16),
            pltpu.VMEM(ROWS, f32),
            pltpu.SemaphoreType.DMA((8,)),
            pltpu.SemaphoreType.DMA((MP, 4)),
            pltpu.SemaphoreType.DMA((MP, 4)),
            pltpu.SemaphoreType.DMA((MP, 3)),
            pltpu.SemaphoreType.DMA((2, 4)),
        ],
        compiler_params=params(),
        cost_estimate=cost(20),
        name="ffn_bwd",
    )(flags, gain, *gout, middle, normed, hidden, ga, gb, *ffn_weights, *prev)


def attn_bwd(flags, table, gmid, x, gain, band, ffn_gain, early, normed, qkv, lse, mixed, attn_weights, prev):
    results = [shape(HALF_ROWS, bf16)] * 2 + [shape((1, D), f32)] + [shape((MP, 2, QUARTER + SMALL, D), bf16)] * 2
    prev = prev or []
    held = (gmid, normed, shape((table.shape[1], 4 * BLK), f32), normed, qkv, lse, mixed)
    return pl.pallas_call(
        attn_bwd_kernel,
        in_specs=[smem()] * 2 + [vmem()] * 5 + [hbm()] * (7 + N_CHUNK + len(prev)),
        out_specs=[hbm()] * 5,
        out_shape=results,
        input_output_aliases={14 + N_CHUNK + i: i for i in range(len(prev))},
        scratch_shapes=on_vmem(held)
        + on_vmem([shape(ROWS, bf16), shape((1, D), f32)])
        + [
            pltpu.VMEM((MP, 8, 6 * BLK), f32),
            pltpu.VMEM((MP, D, D), bf16),
            pltpu.VMEM(ROWS, bf16),
            pltpu.VMEM((DOC_LEN, QUARTER), bf16),
            pltpu.VMEM((DOC_LEN, QKV), bf16),
            pltpu.VMEM((2, D, D), bf16),
            pltpu.VMEM(ROWS, f32),
            pltpu.VMEM((2, MP, 2, SMALL, D), bf16),
            pltpu.SemaphoreType.DMA((10,)),
            pltpu.SemaphoreType.DMA((MP, 4)),
            pltpu.SemaphoreType.DMA((MP, 2)),
            pltpu.SemaphoreType.DMA((2, 4)),
            pltpu.SemaphoreType.DMA((2,)),
        ],
        compiler_params=params(),
        cost_estimate=cost(25),
        name="attn_bwd",
    )(flags, table, table, gain, band, ffn_gain, early, gmid, *x, normed, qkv, lse, mixed, *attn_weights, *prev)


def swap(values, axis, bit):
    count = lax.axis_size(axis)
    return lax.ppermute(values, axis, [(i, i ^ bit) for i in range(count)])


def swap_cores(values, axis, bit, core):
    dp_count, mp_count = lax.axis_size("dp"), lax.axis_size("mp")
    perm = []
    for i in range(core, dp_count, 2):
        for j in range(mp_count):
            to = (i ^ bit) * mp_count + j if axis == "dp" else i * mp_count + (j ^ bit)
            perm.append((i * mp_count + j, to))
    return lax.ppermute(values, ("dp", "mp"), perm)


def hop(rows, source):
    first = lax.ppermute(rows[0], "section", [(source, 1 - source)])
    dp_count = lax.axis_size("dp")
    perm = [(source * dp_count + i, (1 - source) * dp_count + i) for i in range(0, dp_count, 2)]
    return first, lax.ppermute(rows[1], ("section", "dp"), perm)


def pick(values, axis, index):
    return lax.dynamic_index_in_dim(values, index, axis, keepdims=False)


def add_low(a, b):
    return (a.astype(f32) + b.astype(f32)).astype(bf16)


def fence(*values):
    return lax.optimization_barrier(values)


def total_of(terms, more=()):
    def part(array, picks):
        for dim, index in picks:
            array = pick(array, dim, index)
        return array.astype(f32)

    return functools.reduce(jnp.add, [part(array, picks + more) for array, picks in terms]).astype(bf16)


def give(terms, dim, axis, bit, mine):
    return swap(total_of(terms, ((dim, 1 - mine),)), axis, bit)


def take(terms, dim, mine, got):
    return [(array, picks + ((dim, mine),)) for array, picks in terms] + [(got, ())]


def fence_terms(terms, *values):
    arrays, values = lax.optimization_barrier(([[array for array, _ in one] for one in terms], values))
    terms = [[(array, picks) for array, (_, picks) in zip(new, old)] for new, old in zip(arrays, terms)]
    return *terms, *values


def in_order(mine, values, other):
    return jnp.where(mine == 0, jnp.stack([values, other]), jnp.stack([other, values]))


def over_rest(total):
    bit = 4
    while bit < lax.axis_size("dp"):
        total = add_low(total, swap(total, "dp", bit))
        bit *= 2
    return total


def spread_tokens(tokens, place, pairs):
    z = place[2]
    got = []
    for turn in range(2):
        perm = []
        for j in range(pairs):
            for c in range(2):
                for zz in range(MP):
                    u = (turn + zz) % 2
                    perm.append(((2 * j + c) * MP + zz, (2 * j + zz // 2) * MP + 2 * c + u))
        block = pick(tokens, 0, (turn + z) % 2)
        got.append(lax.ppermute(block, ("dp", "mp"), perm))
    return got


def arrange_tokens(got, place):
    core, _, z = place
    low, high = jnp.where(z % 2 == 0, jnp.stack(got), jnp.stack(got[::-1]))
    cut = DOC_LEN - 2 * QUARTER
    tail = swap(low[:cut], "dp", 1)
    doc = jnp.concatenate([low, high, tail])
    qry = jnp.concatenate([low[cut:], high, jnp.zeros((DOC_LEN - QRY_ROWS, D), low.dtype)])
    rows = jnp.where(core == 0, doc, qry)
    return rows[:QRY_ROWS], rows[QRY_ROWS:]


def split_rows(rows, place):
    core = place[0]
    cut = DOC_LEN - 2 * QUARTER
    tail = swap(rows[2 * QUARTER :], "dp", 1)
    low_q = jnp.concatenate([tail, rows[: QUARTER - cut]])
    high_q = rows[QUARTER - cut : QRY_ROWS]
    low = jnp.where(core == 0, rows[:QUARTER], low_q)
    high = jnp.where(core == 0, rows[QUARTER : 2 * QUARTER], high_q)
    return low, high


def collect_rows(blocks, place, pairs):
    low, high = blocks
    z = place[2]
    got = []
    for turn in range(2):
        perm = []
        for j in range(pairs):
            for c in range(2):
                for zz in range(MP):
                    u = (turn + zz) % 2
                    perm.append(((2 * j + zz // 2) * MP + 2 * c + u, (2 * j + c) * MP + zz))
        block = jnp.where((z + turn) % 2 == 0, low, high)
        got.append(lax.ppermute(block, ("dp", "mp"), perm))
    return jnp.where(z % 2 == 0, jnp.stack(got), jnp.stack(got[::-1]))


def gather_slots(values, steps, core):
    for axis, bit in steps:
        values = jnp.concatenate([values, swap_cores(values, axis, bit, core)])
    return values


def scatter_slots(values, steps, core):
    for axis, bit in reversed(steps):
        half = values.shape[0] // 2
        values = add_low(values[:half], swap_cores(values[half:], axis, bit, core))
    return values[0]


def on_device(
    tokens,
    attn_gain,
    w_query,
    w_key,
    w_value,
    w_out,
    ffn_gain,
    w_gate,
    w_up,
    w_down,
    rel_table,
    final_gain,
    w_proj,
    positives,
    retrieved,
):
    section = lax.axis_index("section")
    dp = lax.axis_index("dp")
    dp_count = lax.axis_size("dp")
    z = lax.axis_index("mp")
    core, y = dp % 2, (dp // 2) % 2
    place = (core, y, z)
    pairs = dp_count // 2
    chip = (dp // 2) * MP + z
    chips = pairs * MP
    is_doc = core == 0
    first = section == 0
    quad = dp % 4

    def piece_of(quarter):
        return lax.dynamic_slice_in_dim(quarter, quad * QUARTER, QUARTER, 0)

    attn_own = jnp.concatenate([w_query[0].T, w_key[0].T, w_value[0].T, w_out[0]])
    def ffn_owns(gate, up, down):
        whole = jnp.concatenate([gate[0], up[0], down[0].T], axis=1)
        return [whole[:, :F_HALF], whole[:, F_HALF:]]

    owns = [attn_own]
    own_pieces = [piece_of(attn_own)]
    got = {}

    def along_z(k, *which):
        for at in which:
            source = own_pieces[k] if at < 3 else got[k, 2, 0]
            got[k, at, 0] = swap(source, "mp", 1 if at == 3 else at)

    def along_y(k, *which):
        for at in which:
            got[k, at, 1] = swap(got[k, at, 0], "dp", 2)

    def to_core(k, m, *which):
        for at in which:
            got[k, at, 2 + m] = swap(got[k, at, m], "dp", 1)

    def hold(keys, *values):
        held, values = lax.optimization_barrier(([got[key] for key in keys], values))
        got.update(zip(keys, held))
        return values

    def chunk_of(k):
        return (owns[k],) + tuple(got[k, at, m] for at in range(1, MP) for m in range(4))

    heads_dev = rel_table.shape[1]
    buckets = rel_table.shape[0]
    half_count = buckets // 2
    bucket_ids = jnp.arange(buckets, dtype=jnp.int32)

    def flags_for(active):
        return jnp.stack([jnp.asarray(active).astype(jnp.int32), is_doc.astype(jnp.int32), z, quad])

    def whole_table(table):
        table = jnp.take(jnp.stack(table), z ^ jnp.arange(MP), axis=0, mode="clip")
        return jnp.swapaxes(table, 0, 1).reshape(buckets, -1)

    def band_picks(lanes):
        band_offset = jnp.where(lanes <= 2 * BLK + BLK - 1, BLK - lanes, 5 * BLK - lanes)
        ends = [jnp.full((BLK,), buckets - 1, jnp.int32), jnp.full((BLK,), half_count - 1, jnp.int32)]
        band_bucket = jnp.concatenate([bucket_of(band_offset, half_count)] + ends)
        return (band_bucket[:, None] == jnp.arange(BLK, dtype=jnp.int32)).astype(f32)

    topk = retrieved.shape[2]
    mb_of_slot = chip ^ jnp.arange(chips, dtype=jnp.int32)

    def counts_of(hits):
        hits = jnp.take(jnp.concatenate(hits), dp ^ jnp.arange(dp_count), axis=0, mode="clip").reshape(chips * QRYS_MB, -1)
        slot_retrieved = jnp.take(hits[:, : QRY_LEN * topk].reshape(chips, QRY_ROWS, topk), mb_of_slot, axis=0, mode="clip")
        flags = flags_for(jnp.logical_not(first))
        positives_slot = jnp.take(
            hits[:, QRY_LEN * topk :].reshape(chips, QRYS_MB, -1), mb_of_slot, axis=0, mode="clip"
        ).reshape(chips * QRYS_MB, -1)
        chosen = jnp.any(positives_slot[None] == mb_of_slot[:, None, None], axis=2).astype(f32)
        return chosen, count_hits(flags, slot_retrieved.reshape(-1, topk).T - chip * DOC_LEN)

    along_z(0, 2, 1)
    table = [rel_table] + [swap(rel_table, "mp", by) for by in range(1, MP)]
    w_gate, w_up, w_down, tokens, table, retrieved, positives = hold(
        [(0, 1, 0), (0, 2, 0)], w_gate, w_up, w_down, tokens, table, retrieved, positives
    )
    along_z(0, 3)
    along_y(0, 1, 2)
    to_core(0, 0, 1, 2)
    tokens = spread_tokens(tokens, place, pairs)
    owns += ffn_owns(w_gate, w_up, w_down)
    own_pieces += [piece_of(own) for own in owns[1:]]
    owns, own_pieces, tokens, table, retrieved, positives = hold(
        [(0, 3, 0), (0, 1, 1), (0, 2, 1)], owns, own_pieces, tokens, table, retrieved, positives
    )
    along_y(0, 3)
    to_core(0, 0, 3)
    to_core(0, 1, 1, 2)
    along_z(1, 2, 1)
    x_first = arrange_tokens(tokens, place)
    table = whole_table(table)
    x_first, table, own_pieces[2], retrieved, positives = hold(
        [(0, 3, 1), (1, 1, 0), (1, 2, 0)], x_first, table, own_pieces[2], retrieved, positives
    )
    hits = jnp.concatenate([retrieved.reshape(retrieved.shape[0], -1), positives], axis=1)[None]
    hits = [hits] + [swap(hits, "dp", by) for by in range(1, dp_count)]
    lanes = jnp.arange(chips * QRY_ROWS, dtype=jnp.int32)
    to_core(0, 1, 3)
    along_z(1, 3)
    along_z(2, 2, 1)
    along_y(1, 1, 2)
    to_core(1, 0, 1, 2)
    attn_weights = chunk_of(0)

    kept = []
    x = x_first
    for step in range(2):
        flags = flags_for(section == step)
        normed, qkv, lse, mixed, middle, normed_ffn = attn_fwd(flags, table, x, attn_gain, ffn_gain, attn_weights)
        if step == 0:
            middle, normed_ffn, hits, lanes = hold(
                [(1, 3, 0), (1, 1, 1), (1, 2, 1), (2, 1, 0), (2, 2, 0)], middle, normed_ffn, hits, lanes
            )
            along_z(2, 3)
            along_y(2, 1, 2)
            along_y(1, 3)
            to_core(1, 0, 3)
            to_core(1, 1, 1, 2)
            to_core(2, 0, 1, 2)
            chosen, counts = counts_of(hits)
            expand = (lanes // QRY_LEN == jnp.arange(chips * QRYS_MB)[:, None]).astype(f32)
            chosen, counts, expand, pick_band = hold(
                [(2, 3, 0), (2, 1, 1), (2, 2, 1), (1, 3, 1)], chosen, counts, expand, band_picks(lanes[: 4 * BLK])
            )
            along_y(2, 3)
            to_core(1, 1, 3)
            to_core(2, 0, 3)
            to_core(2, 1, 1, 2)
            hold([(2, 3, 1)])
            to_core(2, 1, 3)
            ffn_weights = chunk_of(1) + chunk_of(2)
        out, low, low_high, hidden, ga, gb, normed_final, embed = ffn_fwd(
            flags, final_gain[None], w_proj, middle, normed_ffn, ffn_weights
        )
        kept.append((x, normed, qkv, lse, mixed, middle, normed_ffn, hidden, ga, gb))
        if step == 0:
            x = hop((low, low_high), 0)

    live = jnp.logical_not(first)
    scale = PROJ ** (-0.5)
    steps = [("mp", 1), ("mp", 2)]
    bit = 2
    while bit < dp_count:
        steps.append(("dp", bit))
        bit *= 2
    query_slots = swap(gather_slots(embed[None, :QRY_ROWS], steps, 1), "dp", 1).reshape(-1, PROJ)
    shares, share_query, mass = score(flags_for(live), query_slots, embed, counts)
    logit = logit_scale * jnp.mean(jnp.log1p(mass).reshape(chips * QRYS_MB, QRY_LEN), axis=1)
    logits = logit[None]
    for at, (axis, bit) in enumerate(steps):
        got_logits = swap_cores(logits, axis, bit, 0)
        turned = got_logits.reshape(got_logits.shape[0], -1, 2, QRYS_MB << at)[:, :, ::-1]
        logits = jnp.concatenate([logits, turned.reshape(got_logits.shape)])
    coef, grad_query, loss_here = coefs(flags_for(live), logits, chosen, expand, share_query)
    grad_query = scatter_slots(swap(grad_query.reshape(chips, QRY_ROWS, PROJ), "dp", 1), steps, 1)
    lead = jnp.logical_and(live, jnp.logical_and(dp == 0, z == 0))
    loss_here = jnp.where(lead, loss_here, 0.0)
    *grad_final, early_own = head_bwd(
        flags_for(live), shares, query_slots, coef, grad_query, loss_here, normed_final, out, final_gain[None], w_proj
    )
    early = (early_own + swap(early_own, "section", 1)).astype(f32)

    def ffn_back(step, grad_out, prev):
        x, normed, qkv, lse, mixed, middle, normed_ffn, hidden, ga, gb = kept[step]
        flags = flags_for(section == step)
        return ffn_bwd(flags, grad_out, middle, ffn_gain, normed_ffn, hidden, ga, gb, ffn_weights, prev)

    def attn_back(step, gmid, ffn_gain_grad, prev):
        x, normed, qkv, lse, mixed, middle, normed_ffn, hidden, ga, gb = kept[step]
        flags = flags_for(section == step)
        return attn_bwd(
            flags, table, gmid, x, attn_gain, pick_band, ffn_gain_grad, early, normed, qkv, lse, mixed, attn_weights, prev
        )

    gmid, *ffn_prev = ffn_back(1, grad_final, None)
    attn_prev = attn_back(1, gmid, ffn_prev[0], None)
    gmid, grad_ffn_gain, f1_keep, f1_send, f2_keep, f2_send = ffn_back(0, hop(attn_prev[:2], 1), ffn_prev)

    zl, zh = z % 2, z // 2

    def parts(values):
        return values.reshape(2, 2, 2, -1, values.shape[-1])

    def both(keep, send):
        return [(parts(keep), ()), (parts(swap(send, "dp", 1)), ())]

    f1, f2, gmid = fence_terms((both(f1_keep, f1_send), both(f2_keep, f2_send)), gmid)
    f1_got = give(f1, 2, "dp", 2, y)
    f2_got = give(f2, 1, "mp", 1, zl)
    gx, gx_high, _, a_keep, a_send = attn_back(0, gmid, grad_ffn_gain, attn_prev)
    f1, f2, f1_got, f2_got, a_keep, a_send, gx = fence_terms((f1, f2), f1_got, f2_got, a_keep, a_send, gx)
    f1, f2 = take(f1, 2, y, f1_got), take(f2, 1, zl, f2_got)
    out_f1, out_f2 = total_of(f1, ((1, 1 - zl),)), total_of(f2, ((0, 1 - zh),))
    n_small = SMALL - 8
    a = both(a_keep, a_send)
    a, out_f1, out_f2 = fence_terms((a,), out_f1, out_f2)
    f1_got, f2_got = swap(out_f1, "mp", 1), swap(out_f2, "mp", 2)
    a_got = give(a, 2, "dp", 2, y)
    f1, f2, a, f1_got, f2_got, a_got, gx = fence_terms((f1, f2, a), f1_got, f2_got, a_got, gx)

    blocks = split_rows(jnp.concatenate([gx, gx_high]), place)
    f1, f2, a = take(f1, 1, zl, f1_got), take(f2, 0, zh, f2_got), take(a, 2, y, a_got)
    a_got = give(a, 1, "mp", 1, zl)
    f1_got = give(f1, 0, "mp", 2, zh)
    f2 = total_of(f2)
    f2_got = swap(f2, "dp", 2)

    a = take(a, 1, zl, a_got)
    a_got = give(a, 0, "mp", 2, zh)
    f1 = over_rest(total_of(take(f1, 0, zh, f1_got)))
    f1_got = swap(f1, "dp", 2)
    f2 = over_rest(add_low(f2, f2_got))
    f2_other = swap(f2, "dp", 1)

    a, blocks = fence(over_rest(total_of(take(a, 0, zh, a_got))), blocks)
    a_got = swap(a, "dp", 2)
    d_inputs = collect_rows(blocks, place, pairs)[None]
    f1 = in_order(y, f1, f1_got)
    f1_other = swap(f1, "dp", 1)
    flags_end = flags_for(1)
    ffn_sums = finish(finish_ffn_kernel, flags_end, [(D, FQ), (D, FQ), (FQ, D)], f1, f1_other, f2, f2_other)

    a, a_got, d_inputs = fence(a, a_got, d_inputs)
    small_sum = a[QUARTER : QUARTER + n_small].astype(f32)
    table_other = swap(small_sum[:heads_dev], "section", 1)
    a = in_order(y, a, a_got)
    a_other = swap(a, "dp", 1)
    attn_sums = finish(finish_attn_kernel, flags_end, [(QUARTER, D)] * 4, a, a_other)
    proj_sum = in_order(core, a[:, QUARTER + n_small :], a_other[:, QUARTER + n_small :])
    proj_sum = proj_sum.astype(f32).reshape(PROJ // MP, D)
    shared_sum = small_sum[heads_dev:]
    grad_table = (small_sum[:heads_dev] + table_other)[:, :buckets].T
    return (
        shared_sum[3, 0] + shared_sum[4, 0],
        d_inputs,
        shared_sum[0:1],
        attn_sums[0].T[None],
        attn_sums[1].T[None],
        attn_sums[2].T[None],
        attn_sums[3][None],
        shared_sum[1:2],
        ffn_sums[0][None],
        ffn_sums[1][None],
        ffn_sums[2][None],
        grad_table,
        shared_sum[2],
        proj_sum.T,
    )


def solution(mesh):
    return jax.shard_map(
        on_device,
        mesh=mesh,
        in_specs=(
            P("dp", "mp", None),
            P("section", None),
            P("section", None, "mp"),
            P("section", None, "mp"),
            P("section", None, "mp"),
            P("section", "mp", None),
            P("section", None),
            P("section", None, "mp"),
            P("section", None, "mp"),
            P("section", "mp", None),
            P(None, "mp"),
            P(),
            P(),
            P("dp", None),
            P("dp", None, None),
        ),
        out_specs=(
            P(),
            P("section", "dp", "mp", None),
            P("section", None),
            P("section", None, "mp"),
            P("section", None, "mp"),
            P("section", None, "mp"),
            P("section", "mp", None),
            P("section", None),
            P("section", None, "mp"),
            P("section", None, "mp"),
            P("section", "mp", None),
            P(None, "mp"),
            P(),
            P(None, "mp"),
        ),
        check_vma=False,
    )
```

profile of v0, /device:TPU:8, one launch (start us, length us, event | category | flops | bytes accessed | tf_op | source)
XLA Modules:
  0.0 459.9 jit_solution(5839528569877832743)
XLA Ops:
  9.9 7.4 %collective-permute-done.2 = f32[32,3]{0,1:T(4,128)S(1)} collective-permute-done((f32[32,3]{0,1:T(4,128)S(1)}, f32[32,3]{0,1:T(4,128)S(1)}, u32[]{:S(2)}, u32[]{:S(2)}) %collective-permute-start.2) | collective-permute-done | bytes 416 | tf_op jit(solution)/shard_map/ppermute | solution.py:929
  27.8 10.1 %collective-permute-start.19 = (bf16[192,768]{1,0:T(8,128)(2,1)S(1)}, bf16[192,768]{1,0:T(8,128)(2,1)S(1)}, u32[]{:S(2)}, u32[]{:S(2)}) collective-permute-start(bf16[192,768]{1,0:T(8,128)(2,1)S(1)} %copy-done.37), channel_id=1, source_target_pairs={{0,4},{4,0},{8,12},{12,8},{1,5},{5,1},{9,13},{13,9},{2,6},{6,2},{1... | collective-permute-start | bytes 884744 | tf_op jit(solution)/shard_map/ppermute | solution.py:929
  37.9 3.9 collective-permute-start.21
  43.5 3.4 collective-permute-start.12
  47.2 4.6 collective-permute-done.10.refs_10_
  51.8 3.4 collective-permute-done.11.refs_1_
  71.1 16.2 %attn_fwd.2 = (bf16[512,768]{1,0:T(8,128)(2,1)}, bf16[4,512,576]{2,1,0:T(8,128)(2,1)}, f32[4,8,512]{2,1,0:T(8,128)}, bf16[4,512,192]{2,1,0:T(8,128)(2,1)}, f32[512,768]{1,0:T(8,128)}, /*index=5*/bf16[512,768]{1,0:T(8,128)(2,1)}) custom-call(s32[4]{0:T(128)} %add_add_fusion.flags, f32[32,12]{1,0:T(8,128)} %copy.67.table.table_ref, ...), custom_call_target="tpu_custom_call" | custom-call | flops 14000000000 | bytes 16777216 | tf_op jit(solution)/shard_map/attn_fwd/pallas_call | solution.py:696
  100.0 7.3 %collective-permute-done.29.refs_15_ = bf16[192,768]{1,0:T(8,128)(2,1)S(1)} collective-permute-done((bf16[192,768]{1,0:T(8,128)(2,1)S(1)}, bf16[192,768]{1,0:T(8,128)(2,1)S(1)}, u32[]{:S(2)}, u32[]{:S(2)}) %collective-permute-start.29) | collective-permute-done | bytes 294944 | tf_op jit(solution)/shard_map/ppermute | solution.py:929
  107.3 5.6 %collective-permute-done.31.refs_10_ = bf16[192,768]{1,0:T(8,128)(2,1)S(1)} collective-permute-done((bf16[192,768]{1,0:T(8,128)(2,1)S(1)}, bf16[192,768]{1,0:T(8,128)(2,1)S(1)}, u32[]{:S(2)}, u32[]{:S(2)}) %collective-permute-start.31) | collective-permute-done | bytes 294944 | tf_op jit(solution)/shard_map/ppermute | solution.py:929
  114.7 6.8 %collective-permute-done.42.refs_23_ = bf16[192,768]{1,0:T(8,128)(2,1)S(1)} collective-permute-done((bf16[192,768]{1,0:T(8,128)(2,1)}, bf16[192,768]{1,0:T(8,128)(2,1)S(1)}, u32[]{:S(2)}, u32[]{:S(2)}) %collective-permute-start.42) | collective-permute-done | bytes 294944 | tf_op jit(solution)/shard_map/ppermute | solution.py:929
  126.5 12.5 %ffn_fwd.2 = (f32[512,768]{1,0:T(8,128)}, bf16[256,768]{1,0:T(8,128)(2,1)}, bf16[256,768]{1,0:T(8,128)(2,1)}, bf16[4,512,512]{2,1,0:T(8,128)(2,1)}, bf16[4,512,5...) custom-call(s32[4]{0:T(128)} %add_add_fusion.flags, ...), custom_call_target="tpu_custom_call" | custom-call | flops 10000000000 | bytes 16777216 | tf_op jit(solution)/shard_map/ffn_fwd/pallas_call | solution.py:718
  142.3 4.9 %collective-permute-done.45.x_low = bf16[256,768]{1,0:T(8,128)(2,1)S(1)} collective-permute-done((bf16[256,768]{1,0:T(8,128)(2,1)}, bf16[256,768]{1,0:T(8,128)(2,1)S(1)}, u32[]{:S(2)}, u32[]{:S(2)}) %collective-permute-start.45) | collective-permute-done | bytes 393248 | tf_op jit(solution)/shard_map/ppermute | solution.py:943
  147.3 4.2 collective-permute-done.46.x_high
  158.5 10.6 %collective-permute-start.50 = (bf16[8,256,128]{2,1,0:T(8,128)(2,1)S(1)}, bf16[8,256,128]{2,1,0:T(8,128)(2,1)S(1)}, u32[]{:S(2)}, u32[]{:S(2)}) collective-permute-start(bf16[8,256,128]{2,1,0:T(8,128)(2,1)S(1)} %pad_maximum_fusion.3), channel_id=1, source_target_pairs={{0,4},{4,0},{8,12},{12,8},{1,5},{5,1},{9,13},{13,9},{2,6},{6,2},{1... | collective-permute-start | bytes 1572872 | tf_op jit(solution)/shard_map/ppermute | solution.py:929
  171.4 4.2 score.1
  176.6 3.7 collective-permute-start.51
  183.4 3.5 collective-permute-start.52
  204.1 3.5 head_bwd.1
  207.6 26.7 %collective-permute-start.58 = (bf16[144,768]{1,0:T(8,128)(2,1)}, bf16[144,768]{1,0:T(8,128)(2,1)S(1)}, u32[]{:S(2)}, u32[]{:S(2)}) collective-permute-start(bf16[144,768]{1,0:T(8,128)(2,1)} %get-tuple-element.245), channel_id=1, source_target_pairs={{0,16},{16,0},{1,17},{17,1},{2,18},{18,2},{3,19},{19,3},{4,20},{20... | collective-permute-start | bytes 663560 | tf_op jit(solution)/shard_map/ppermute | solution.py:929
  239.2 7.2 %attn_bwd.2 = (bf16[256,768]{1,0:T(8,128)(2,1)}, bf16[256,768]{1,0:T(8,128)(2,1)}, f32[1,768]{1,0:T(1,128)}, bf16[4,2,208,768]{3,2,1,0:T(8,128)(2,1)}, bf16[4,2,208,768]{3,2,1,0:T(8,128)(2,1)}) custom-call(s32[4]{0:T(128)} %add_add_fusion.1.flags, f32[32,12]{1,0:T(8,128)} %copy.67.table.table_ref, f32[32,12]{1,0:T(8,128)} %copy.67.table.table_ref, ...), custom_call_target="tpu_custom_call" | custom-call | flops 24999999488 | bytes 16777216 | tf_op jit(solution)/shard_map/attn_bwd/pallas_call | solution.py:898
  249.0 35.6 %collective-permute-done.59.gout_low = bf16[256,768]{1,0:T(8,128)(2,1)S(1)} collective-permute-done((bf16[256,768]{1,0:T(8,128)(2,1)}, bf16[256,768]{1,0:T(8,128)(2,1)S(1)}, u32[]{:S(2)}, u32[]{:S(2)}) %collective-permute-start.59) | collective-permute-done | bytes 393248 | tf_op jit(solution)/shard_map/ppermute | solution.py:943
  284.6 7.4 %collective-permute-done.60.gout_high = bf16[256,768]{1,0:T(8,128)(2,1)S(1)} collective-permute-done((bf16[256,768]{1,0:T(8,128)(2,1)}, bf16[256,768]{1,0:T(8,128)(2,1)S(1)}, u32[]{:S(2)}, u32[]{:S(2)}) %collective-permute-start.60) | collective-permute-done | bytes 393248 | tf_op jit(solution)/shard_map/ppermute | solution.py:946
  292.7 16.9 %ffn_bwd.3 = (f32[512,768]{1,0:T(8,128)}, f32[1,768]{1,0:T(1,128)}, bf16[4,384,768]{2,1,0:T(8,128)(2,1)}, bf16[4,384,768]{2,1,0:T(8,128)(2,1)}, bf16[4,384,768]{...) custom-call(s32[4]{0:T(128)} %add_add_fusion.flags, ...), custom_call_target="tpu_custom_call", output_to_operand_aliasing={{1}: (35, {}), {2}: (36, {}), {3}: (37, {}), {4}: (38, {}),... | custom-call | flops 20000000000 | bytes 16777216 | tf_op jit(solution)/shard_map/ffn_bwd/pallas_call | solution.py:868
  310.3 6.8 %collective-permute-done.61 = bf16[4,384,768]{2,1,0:T(8,128)(2,1)S(1)} collective-permute-done((bf16[4,384,768]{2,1,0:T(8,128)(2,1)}, bf16[4,384,768]{2,1,0:T(8,128)(2,1)S(1)}, u32[]{:S(2)}, u32[]{:S(2)}) %collective-permute-start.61) | collective-permute-done | bytes 2359328 | tf_op jit(solution)/shard_map/ppermute | solution.py:929
  323.5 24.3 %attn_bwd.3 = (bf16[256,768]{1,0:T(8,128)(2,1)}, bf16[256,768]{1,0:T(8,128)(2,1)}, f32[1,768]{1,0:T(1,128)}, bf16[4,2,208,768]{3,2,1,0:T(8,128)(2,1)}, bf16[4,2,208,768]{3,2,1,0:T(8,128)(2,1)}) custom-call(s32[4]{0:T(128)} %add_add_fusion.flags, ...), custom_call_target="tpu_custom_call", output_to_operand_aliasing={{0}: (27, {}), {1}: (28, {}), {2}: (29, {}), {3}: (30, {}),... | custom-call | flops 24999999488 | bytes 16777216 | tf_op jit(solution)/shard_map/attn_bwd/pallas_call | solution.py:898
  360.6 23.0 %collective-permute-done.66 = bf16[2,192,768]{2,1,0:T(8,128)(2,1)} collective-permute-done((bf16[2,192,768]{2,1,0:T(8,128)(2,1)}, bf16[2,192,768]{2,1,0:T(8,128)(2,1)}, u32[]{:S(2)}, u32[]{:S(2)}) %collective-permute-start.66) | collective-permute-done | bytes 589856 | tf_op jit(solution)/shard_map/ppermute | solution.py:929
  395.9 15.3 %collective-permute-done.76 = bf16[192,768]{1,0:T(8,128)(2,1)S(1)} collective-permute-done((bf16[192,768]{1,0:T(8,128)(2,1)S(1)}, bf16[192,768]{1,0:T(8,128)(2,1)S(1)}, u32[]{:S(2)}, u32[]{:S(2)}) %collective-permute-start.76) | collective-permute-done | bytes 294944 | tf_op jit(solution)/shard_map/ppermute | solution.py:929
  415.4 4.5 collective-permute-done.77
  420.1 7.2 %collective-permute-done.70 = bf16[208,768]{1,0:T(8,128)(2,1)S(1)} collective-permute-done((bf16[208,768]{1,0:T(8,128)(2,1)S(1)}, bf16[208,768]{1,0:T(8,128)(2,1)S(1)}, u32[]{:S(2)}, u32[]{:S(2)}) %collective-permute-start.70) | collective-permute-done | bytes 319520 | tf_op jit(solution)/shard_map/ppermute | solution.py:929
  429.4 3.6 collective-permute-start.74
  436.1 4.3 finish.3
  443.9 5.2 %collective-permute-start.75 = (bf16[2,208,768]{2,1,0:T(8,128)(2,1)S(1)}, bf16[2,208,768]{2,1,0:T(8,128)(2,1)S(1)}, u32[]{:S(2)}, u32[]{:S(2)}) collective-permute-start(bf16[2,208,768]{2,1,0:T(8,128)(2,1)S(1)} %maximum_select_fusion.1.mine), channel_id=1, source_target_pairs={{0,4},{4,0},{8,12},{12,8},{1,5},{5,1},{9,13},{13,9},{2,6},{6,2},{1... | collective-permute-start | bytes 1916936 | tf_op jit(solution)/shard_map/ppermute | solution.py:929
  (399 shorter events, 151.2 us)
Async XLA Ops:
  2.1 16.5 %collective-permute-start = (bf16[192,768]{1,0:T(8,128)(2,1)S(1)}, bf16[192,768]{1,0:T(8,128)(2,1)S(1)}, u32[]{:S(2)}, u32[]{:S(2)}) collective-permute-start(bf16[192,768]{1,0:T(8,128)(2,1)S(1)} %constant_dynamic-slice_fusion), channel_id=1, source_target_pairs={{0,1},{1,0},{2,3},{3,2},{4,5},{5,4},{6,7},{7,6},{8,9},{9,8},{10,11... | collective-permute-start | bytes 884744 | tf_op jit(solution)/shard_map/ppermute | solution.py:929
  2.1 16.5 %collective-permute-start.1 = (bf16[192,768]{1,0:T(8,128)(2,1)S(1)}, bf16[192,768]{1,0:T(8,128)(2,1)}, u32[]{:S(2)}, u32[]{:S(2)}) collective-permute-start(bf16[192,768]{1,0:T(8,128)(2,1)S(1)} %constant_dynamic-slice_fusion), channel_id=1, source_target_pairs={{0,2},{1,3},{2,0},{3,1},{4,6},{5,7},{6,4},{7,5},{8,10},{9,11},{10,... | collective-permute-start | bytes 884744 | tf_op jit(solution)/shard_map/ppermute | solution.py:929
  18.6 23.2 %collective-permute-start.5 = (bf16[192,768]{1,0:T(8,128)(2,1)}, bf16[192,768]{1,0:T(8,128)(2,1)}, u32[]{:S(2)}, u32[]{:S(2)}) collective-permute-start(bf16[192,768]{1,0:T(8,128)(2,1)} %collective-permute-done.1.refs_5_), channel_id=1, source_target_pairs={{0,1},{1,0},{2,3},{3,2},{4,5},{5,4},{6,7},{7,6},{8,9},{9,8},{10,11... | collective-permute-start | bytes 884744 | tf_op jit(solution)/shard_map/ppermute | solution.py:929
  20.2 21.6 %collective-permute-start.7 = (bf16[192,768]{1,0:T(8,128)(2,1)}, bf16[192,768]{1,0:T(8,128)(2,1)}, u32[]{:S(2)}, u32[]{:S(2)}) collective-permute-start(bf16[192,768]{1,0:T(8,128)(2,1)} %collective-permute-done.1.refs_5_), channel_id=1, source_target_pairs={{0,8},{4,12},{8,0},{12,4},{1,9},{5,13},{9,1},{13,5},{2,10},{6,14},... | collective-permute-start | bytes 884744 | tf_op jit(solution)/shard_map/ppermute | solution.py:929
  25.0 12.9 %collective-permute-start.9 = (bf16[192,768]{1,0:T(8,128)(2,1)S(1)}, bf16[192,768]{1,0:T(8,128)(2,1)S(1)}, u32[]{:S(2)}, u32[]{:S(2)}) collective-permute-start(bf16[192,768]{1,0:T(8,128)(2,1)S(1)} %get-tuple-element.330), channel_id=1, source_target_pairs={{0,1},{1,0},{2,5},{3,4},{4,3},{5,2},{6,7},{7,6},{8,9},{9,8},{10,13... | collective-permute-start | bytes 884744 | tf_op jit(solution)/shard_map/ppermute | solution.py:1007
  25.6 16.2 %collective-permute-start.6 = (bf16[192,768]{1,0:T(8,128)(2,1)}, bf16[192,768]{1,0:T(8,128)(2,1)S(1)}, u32[]{:S(2)}, u32[]{:S(2)}) collective-permute-start(bf16[192,768]{1,0:T(8,128)(2,1)} %copy-done.36), channel_id=1, source_target_pairs={{0,8},{4,12},{8,0},{12,4},{1,9},{5,13},{9,1},{13,5},{2,10},{6,14},... | collective-permute-start | bytes 884744 | tf_op jit(solution)/shard_map/ppermute | solution.py:929
  27.8 32.4 %collective-permute-start.19 = (bf16[192,768]{1,0:T(8,128)(2,1)S(1)}, bf16[192,768]{1,0:T(8,128)(2,1)S(1)}, u32[]{:S(2)}, u32[]{:S(2)}) collective-permute-start(bf16[192,768]{1,0:T(8,128)(2,1)S(1)} %copy-done.37), channel_id=1, source_target_pairs={{0,4},{4,0},{8,12},{12,8},{1,5},{5,1},{9,13},{13,9},{2,6},{6,2},{1... | collective-permute-start | bytes 884744 | tf_op jit(solution)/shard_map/ppermute | solution.py:929
  37.9 22.4 %collective-permute-start.21 = (bf16[192,768]{1,0:T(8,128)(2,1)}, bf16[192,768]{1,0:T(8,128)(2,1)S(1)}, u32[]{:S(2)}, u32[]{:S(2)}) collective-permute-start(bf16[192,768]{1,0:T(8,128)(2,1)} %collective-permute-done.1.refs_5_), channel_id=1, source_target_pairs={{0,4},{4,0},{8,12},{12,8},{1,5},{5,1},{9,13},{13,9},{2,6},{6,2},{1... | collective-permute-start | bytes 884744 | tf_op jit(solution)/shard_map/ppermute | solution.py:929
  43.5 15.8 %collective-permute-start.12 = (bf16[192,768]{1,0:T(8,128)(2,1)S(1)}, bf16[192,768]{1,0:T(8,128)(2,1)S(1)}, u32[]{:S(2)}, u32[]{:S(2)}) collective-permute-start(bf16[192,768]{1,0:T(8,128)(2,1)S(1)} %get-tuple-element.180), channel_id=1, source_target_pairs={{0,2},{1,3},{2,0},{3,1},{4,6},{5,7},{6,4},{7,5},{8,10},{9,11},{10,... | collective-permute-start | bytes 884744 | tf_op jit(solution)/shard_map/ppermute | solution.py:929
  63.6 23.7 %collective-permute-start.14 = (bf16[192,768]{1,0:T(8,128)(2,1)}, bf16[192,768]{1,0:T(8,128)(2,1)S(1)}, u32[]{:S(2)}, u32[]{:S(2)}) collective-permute-start(bf16[192,768]{1,0:T(8,128)(2,1)} %copy-done.44), channel_id=1, source_target_pairs={{0,1},{1,0},{2,3},{3,2},{4,5},{5,4},{6,7},{7,6},{8,9},{9,8},{10,11... | collective-permute-start | bytes 884744 | tf_op jit(solution)/shard_map/ppermute | solution.py:929
  65.9 21.6 %collective-permute-start.16 = (bf16[192,768]{1,0:T(8,128)(2,1)}, bf16[192,768]{1,0:T(8,128)(2,1)S(1)}, u32[]{:S(2)}, u32[]{:S(2)}) collective-permute-start(bf16[192,768]{1,0:T(8,128)(2,1)} %copy-done.44), channel_id=1, source_target_pairs={{0,8},{4,12},{8,0},{12,4},{1,9},{5,13},{9,1},{13,5},{2,10},{6,14},... | collective-permute-start | bytes 884744 | tf_op jit(solution)/shard_map/ppermute | solution.py:929
  67.3 20.2 %collective-permute-start.17 = (bf16[192,768]{1,0:T(8,128)(2,1)S(1)}, bf16[192,768]{1,0:T(8,128)(2,1)S(1)}, u32[]{:S(2)}, u32[]{:S(2)}) collective-permute-start(bf16[192,768]{1,0:T(8,128)(2,1)S(1)} %get-tuple-element.193), channel_id=1, source_target_pairs={{0,1},{1,0},{2,3},{3,2},{4,5},{5,4},{6,7},{7,6},{8,9},{9,8},{10,11... | collective-permute-start | bytes 884744 | tf_op jit(solution)/shard_map/ppermute | solution.py:929
  67.4 20.1 %collective-permute-start.18 = (bf16[192,768]{1,0:T(8,128)(2,1)S(1)}, bf16[192,768]{1,0:T(8,128)(2,1)S(1)}, u32[]{:S(2)}, u32[]{:S(2)}) collective-permute-start(bf16[192,768]{1,0:T(8,128)(2,1)S(1)} %get-tuple-element.193), channel_id=1, source_target_pairs={{0,2},{1,3},{2,0},{3,1},{4,6},{5,7},{6,4},{7,5},{8,10},{9,11},{10,... | collective-permute-start | bytes 884744 | tf_op jit(solution)/shard_map/ppermute | solution.py:929
  70.4 17.0 %collective-permute-start.15 = (bf16[192,768]{1,0:T(8,128)(2,1)}, bf16[192,768]{1,0:T(8,128)(2,1)S(1)}, u32[]{:S(2)}, u32[]{:S(2)}) collective-permute-start(bf16[192,768]{1,0:T(8,128)(2,1)} %collective-permute-done.11.refs_1_), channel_id=1, source_target_pairs={{0,8},{4,12},{8,0},{12,4},{1,9},{5,13},{9,1},{13,5},{2,10},{6,14},... | collective-permute-start | bytes 884744 | tf_op jit(solution)/shard_map/ppermute | solution.py:929
  87.3 26.7 %collective-permute-start.32 = (bf16[192,768]{1,0:T(8,128)(2,1)}, bf16[192,768]{1,0:T(8,128)(2,1)S(1)}, u32[]{:S(2)}, u32[]{:S(2)}) collective-permute-start(bf16[192,768]{1,0:T(8,128)(2,1)} %collective-permute-done.11.refs_1_), channel_id=1, source_target_pairs={{0,4},{4,0},{8,12},{12,8},{1,5},{5,1},{9,13},{13,9},{2,6},{6,2},{1... | collective-permute-start | bytes 884744 | tf_op jit(solution)/shard_map/ppermute | solution.py:929
  90.9 16.4 %collective-permute-start.30 = (bf16[192,768]{1,0:T(8,128)(2,1)}, bf16[192,768]{1,0:T(8,128)(2,1)}, u32[]{:S(2)}, u32[]{:S(2)}) collective-permute-start(bf16[192,768]{1,0:T(8,128)(2,1)} %copy-done.51), channel_id=1, source_target_pairs={{0,8},{4,12},{8,0},{12,4},{1,9},{5,13},{9,1},{13,5},{2,10},{6,14},... | collective-permute-start | bytes 884744 | tf_op jit(solution)/shard_map/ppermute | solution.py:929
  97.1 15.8 %collective-permute-start.31 = (bf16[192,768]{1,0:T(8,128)(2,1)S(1)}, bf16[192,768]{1,0:T(8,128)(2,1)S(1)}, u32[]{:S(2)}, u32[]{:S(2)}) collective-permute-start(bf16[192,768]{1,0:T(8,128)(2,1)S(1)} %collective-permute-done.14.refs_9_), channel_id=1, source_target_pairs={{0,8},{4,12},{8,0},{12,4},{1,9},{5,13},{9,1},{13,5},{2,10},{6,14},... | collective-permute-start | bytes 884744 | tf_op jit(solution)/shard_map/ppermute | solution.py:929
  100.0 14.2 %collective-permute-start.34 = (bf16[192,768]{1,0:T(8,128)(2,1)S(1)}, bf16[192,768]{1,0:T(8,128)(2,1)S(1)}, u32[]{:S(2)}, u32[]{:S(2)}) collective-permute-start(bf16[192,768]{1,0:T(8,128)(2,1)S(1)} %copy-done.45), channel_id=1, source_target_pairs={{0,4},{4,0},{8,12},{12,8},{1,5},{5,1},{9,13},{13,9},{2,6},{6,2},{1... | collective-permute-start | bytes 884744 | tf_op jit(solution)/shard_map/ppermute | solution.py:929
  207.6 30.8 %collective-permute-start.58 = (bf16[144,768]{1,0:T(8,128)(2,1)}, bf16[144,768]{1,0:T(8,128)(2,1)S(1)}, u32[]{:S(2)}, u32[]{:S(2)}) collective-permute-start(bf16[144,768]{1,0:T(8,128)(2,1)} %get-tuple-element.245), channel_id=1, source_target_pairs={{0,16},{16,0},{1,17},{17,1},{2,18},{18,2},{3,19},{19,3},{4,20},{20... | collective-permute-start | bytes 663560 | tf_op jit(solution)/shard_map/ppermute | solution.py:929
  246.4 38.2 %collective-permute-start.59 = (bf16[256,768]{1,0:T(8,128)(2,1)}, bf16[256,768]{1,0:T(8,128)(2,1)S(1)}, u32[]{:S(2)}, u32[]{:S(2)}) collective-permute-start(bf16[256,768]{1,0:T(8,128)(2,1)} %get-tuple-element.251.refs_13_), channel_id=1, source_target_pairs={{16,0},{17,1},{18,2},{19,3},{20,4},{21,5},{22,6},{23,7},{24,8},{25... | collective-permute-start | bytes 1179656 | tf_op jit(solution)/shard_map/ppermute | solution.py:943
  247.7 44.2 %collective-permute-start.60 = (bf16[256,768]{1,0:T(8,128)(2,1)}, bf16[256,768]{1,0:T(8,128)(2,1)S(1)}, u32[]{:S(2)}, u32[]{:S(2)}) collective-permute-start(bf16[256,768]{1,0:T(8,128)(2,1)} %get-tuple-element.252.refs_14_), channel_id=1, source_target_pairs={{16,0},{24,8},{17,1},{25,9},{18,2},{26,10},{19,3},{27,11}} | collective-permute-start | bytes 1179656 | tf_op jit(solution)/shard_map/ppermute | solution.py:946
  320.1 28.1 %collective-permute-start.64 = (bf16[2,2,192,768]{3,2,1,0:T(8,128)(2,1)S(1)}, bf16[2,2,192,768]{3,2,1,0:T(8,128)(2,1)S(1)}, u32[]{:S(2)}, u32[]{:S(2)}) collective-permute-start(bf16[2,2,192,768]{3,2,1,0:T(8,128)(2,1)S(1)} %fusion.3), channel_id=1, source_target_pairs={{0,1},{1,0},{2,3},{3,2},{4,5},{5,4},{6,7},{7,6},{8,9},{9,8},{10,11... | collective-permute-start | bytes 3538952 | tf_op jit(solution)/shard_map/ppermute | solution.py:929
  322.2 27.8 %collective-permute-start.63 = (bf16[2,2,192,768]{3,2,1,0:T(8,128)(2,1)S(1)}, bf16[2,2,192,768]{3,2,1,0:T(8,128)(2,1)S(1)}, u32[]{:S(2)}, u32[]{:S(2)}) collective-permute-start(bf16[2,2,192,768]{3,2,1,0:T(8,128)(2,1)S(1)} %fusion.2), channel_id=1, source_target_pairs={{0,8},{4,12},{8,0},{12,4},{1,9},{5,13},{9,1},{13,5},{2,10},{6,14},... | collective-permute-start | bytes 3538952 | tf_op jit(solution)/shard_map/ppermute | solution.py:929
  357.5 30.4 %collective-permute-start.68 = (bf16[2,2,208,768]{3,2,1,0:T(8,128)(2,1)}, bf16[2,2,208,768]{3,2,1,0:T(8,128)(2,1)}, u32[]{:S(2)}, u32[]{:S(2)}) collective-permute-start(bf16[2,2,208,768]{3,2,1,0:T(8,128)(2,1)} %fusion), channel_id=1, source_target_pairs={{0,8},{4,12},{8,0},{12,4},{1,9},{5,13},{9,1},{13,5},{2,10},{6,14},... | collective-permute-start | bytes 3833864 | tf_op jit(solution)/shard_map/ppermute | solution.py:929
  358.7 25.0 %collective-permute-start.66 = (bf16[2,192,768]{2,1,0:T(8,128)(2,1)}, bf16[2,192,768]{2,1,0:T(8,128)(2,1)}, u32[]{:S(2)}, u32[]{:S(2)}) collective-permute-start(bf16[2,192,768]{2,1,0:T(8,128)(2,1)} %get-tuple-element.291), channel_id=1, source_target_pairs={{0,1},{1,0},{2,3},{3,2},{4,5},{5,4},{6,7},{7,6},{8,9},{9,8},{10,11... | collective-permute-start | bytes 1769480 | tf_op jit(solution)/shard_map/ppermute | solution.py:929
  359.2 27.4 %collective-permute-start.67 = (bf16[2,192,768]{2,1,0:T(8,128)(2,1)S(1)}, bf16[2,192,768]{2,1,0:T(8,128)(2,1)}, u32[]{:S(2)}, u32[]{:S(2)}) collective-permute-start(bf16[2,192,768]{2,1,0:T(8,128)(2,1)S(1)} %get-tuple-element.292), channel_id=1, source_target_pairs={{0,2},{1,3},{2,0},{3,1},{4,6},{5,7},{6,4},{7,5},{8,10},{9,11},{10,... | collective-permute-start | bytes 1769480 | tf_op jit(solution)/shard_map/ppermute | solution.py:929
  360.5 35.2 %collective-permute-start.71 = (bf16[128,768]{1,0:T(8,128)(2,1)S(1)}, bf16[128,768]{1,0:T(8,128)(2,1)S(1)}, u32[]{:S(2)}, u32[]{:S(2)}) collective-permute-start(bf16[128,768]{1,0:T(8,128)(2,1)S(1)} %slice.129), channel_id=1, source_target_pairs={{0,4},{4,0},{8,12},{12,8},{1,5},{5,1},{9,13},{13,9},{2,6},{6,2},{1... | collective-permute-start | bytes 589832 | tf_op jit(solution)/shard_map/ppermute | solution.py:929
  389.4 24.4 %collective-permute-start.69 = (bf16[2,208,768]{2,1,0:T(8,128)(2,1)S(1)}, bf16[2,208,768]{2,1,0:T(8,128)(2,1)S(1)}, u32[]{:S(2)}, u32[]{:S(2)}) collective-permute-start(bf16[2,208,768]{2,1,0:T(8,128)(2,1)S(1)} %fusion.1), channel_id=1, source_target_pairs={{0,1},{1,0},{2,3},{3,2},{4,5},{5,4},{6,7},{7,6},{8,9},{9,8},{10,11... | collective-permute-start | bytes 1916936 | tf_op jit(solution)/shard_map/ppermute | solution.py:929
  392.1 19.1 %collective-permute-start.76 = (bf16[192,768]{1,0:T(8,128)(2,1)S(1)}, bf16[192,768]{1,0:T(8,128)(2,1)S(1)}, u32[]{:S(2)}, u32[]{:S(2)}) collective-permute-start(bf16[192,768]{1,0:T(8,128)(2,1)S(1)} %fusion.11), channel_id=1, source_target_pairs={{0,2},{1,3},{2,0},{3,1},{4,6},{5,7},{6,4},{7,5},{8,10},{9,11},{10,... | collective-permute-start | bytes 884744 | tf_op jit(solution)/shard_map/ppermute | solution.py:929
  394.4 20.7 %collective-permute-start.79 = (bf16[2,192,768]{2,1,0:T(8,128)(2,1)S(1)}, bf16[2,192,768]{2,1,0:T(8,128)(2,1)S(1)}, u32[]{:S(2)}, u32[]{:S(2)}) collective-permute-start(bf16[2,192,768]{2,1,0:T(8,128)(2,1)S(1)} %fusion.5), channel_id=1, source_target_pairs={{0,8},{4,12},{8,0},{12,4},{1,9},{5,13},{9,1},{13,5},{2,10},{6,14},... | collective-permute-start | bytes 1769480 | tf_op jit(solution)/shard_map/ppermute | solution.py:929
  415.3 19.2 %collective-permute-start.80 = (bf16[2,192,768]{2,1,0:T(8,128)(2,1)S(1)}, bf16[2,192,768]{2,1,0:T(8,128)(2,1)S(1)}, u32[]{:S(2)}, u32[]{:S(2)}) collective-permute-start(bf16[2,192,768]{2,1,0:T(8,128)(2,1)S(1)} %add_convert_fusion.3.mine2), channel_id=1, source_target_pairs={{0,4},{4,0},{8,12},{12,8},{1,5},{5,1},{9,13},{13,9},{2,6},{6,2},{1... | collective-permute-start | bytes 1769480 | tf_op jit(solution)/shard_map/ppermute | solution.py:929
  420.0 14.5 %collective-permute-start.78 = (bf16[2,192,768]{2,1,0:T(8,128)(2,1)S(1)}, bf16[2,192,768]{2,1,0:T(8,128)(2,1)S(1)}, u32[]{:S(2)}, u32[]{:S(2)}) collective-permute-start(bf16[2,192,768]{2,1,0:T(8,128)(2,1)S(1)} %maximum_select_fusion.4.mine1), channel_id=1, source_target_pairs={{0,4},{4,0},{8,12},{12,8},{1,5},{5,1},{9,13},{13,9},{2,6},{6,2},{1... | collective-permute-start | bytes 1769480 | tf_op jit(solution)/shard_map/ppermute | solution.py:929
  (121 other events, 905.7 us)
where the time goes:
time: 469 us; the launch traced here: 460 us
  waiting for transfers between devices  178 us (38%)
  starting transfers between devices  125 us (27%)
  Pallas kernels  100 us (21%)
  other arithmetic  30.8 us (7%)
  local copies, waits for them, and re-layouts  21.5 us (5%)
  between operations  4.81 us (1%)
    ppermute x65, waiting for transfers between devices, swap(): return lax.ppermute(values, axis, [(i, i ^ bit) for i in range(count)])  118 us
    ppermute x65, starting transfers between devices, swap(): return lax.ppermute(values, axis, [(i, i ^ bit) for i in range(count)])  100 us
    ppermute x2, waiting for transfers between devices, hop(): first = lax.ppermute(rows[0], 'section', [(source, 1 - source)])  40.5 us
    pallas_call x2, Pallas kernels, attn_bwd(): pl.pallas_call(attn_bwd_kernel, in_specs=[smem()] * 2 + [vmem()] * 5 + [h...  31.5 us
    pallas_call x2, Pallas kernels, ffn_bwd(): pl.pallas_call(ffn_bwd_kernel, in_specs=[smem(), vmem()] + [hbm()] * (7 +...  18.3 us
    pallas_call x2, Pallas kernels, attn_fwd(): pl.pallas_call(attn_fwd_kernel, in_specs=[smem()] * 2 + [vmem()] * 3 + [h...  17.6 us
    convert_element_type x10, other arithmetic, total_of(): functools.reduce(jnp.add, [part(array, picks + more) for array, picks in...  15.5 us
    pallas_call x2, Pallas kernels, ffn_fwd(): pl.pallas_call(ffn_fwd_kernel, in_specs=[smem()] + [vmem()] * 2 + [hbm()]...  14.4 us
  transfers between devices with their start and end apart: 82, of which 40 were waited for; matrix products, arithmetic and copies ran while one was open for 7% of the time, Pallas kernels for 10%

commit v1 on v0

--- a/solution.py
+++ b/solution.py
@@ -32,7 +32,7 @@
 f32 = jnp.float32
 bf16 = jnp.bfloat16
 
-ACT, IS_DOC, ZPOS, RPOS = range(4)
+ACT, IS_DOC, ZPOS, RPOS, LAST = range(5)
 VMEM_LIMIT = 56 * 1024 * 1024
 
 
@@ -320,12 +320,20 @@
         if not doc:
             out_ref[rows:] = jnp.zeros((DOC_LEN - rows, D), f32)
             final_ref[rows:] = jnp.zeros((DOC_LEN - rows, D), bf16)
-        outs = put_rows(copy, low_ref, (low_low, low_high), doc) + [copy(out_ref, out_out)]
-        out = out_ref[:rows]
-        final_ref[:rows] = (out * rms_parts(out) * final_gain_ref[...]).astype(bf16)
-        embed_ref[:rows] = mm(final_ref[:rows], proj_ref[...]).astype(bf16)
-        outs.append(copy(embed_ref.at[pl.ds(0, rows)], embed_out.at[pl.ds(0, rows)]))
-        outs.append(copy(final_ref, final_out))
+        outs = put_rows(copy, low_ref, (low_low, low_high), doc)
+
+        @pl.when(flags[LAST] == 1)
+        def _():
+            out = out_ref[:rows]
+            final_ref[:rows] = (out * rms_parts(out) * final_gain_ref[...]).astype(bf16)
+            embed_ref[:rows] = mm(final_ref[:rows], proj_ref[...]).astype(bf16)
+            lasts = [
+                copy(embed_ref.at[pl.ds(0, rows)], embed_out.at[pl.ds(0, rows)]),
+                copy(out_ref, out_out),
+                copy(final_ref, final_out),
+            ]
+            wait_all(lasts)
+
 
         @pl.loop(0, MP)
         def _(z):
@@ -856,7 +864,7 @@
         out_shape=[pltpu.HBM(r, f32) for r in results],
         scratch_shapes=on_vmem([shape(r, f32) for r in results]) + [pltpu.SemaphoreType.DMA((len(results),))],
         compiler_params=params(),
-        cost_estimate=cost(3),
+        cost_estimate=cost(0.1),
         name="finish",
     )(flags, *values)
 
@@ -1128,7 +1136,7 @@
     bucket_ids = jnp.arange(buckets, dtype=jnp.int32)
 
     def flags_for(active):
-        return jnp.stack([jnp.asarray(active).astype(jnp.int32), is_doc.astype(jnp.int32), z, quad])
+        return jnp.stack([jnp.asarray(active).astype(jnp.int32), is_doc.astype(jnp.int32), z, quad, section])
 
     def whole_table(table):
         table = jnp.take(jnp.stack(table), z ^ jnp.arange(MP), axis=0, mode="clip")

time: 469 us -> 468 us (level)
  transfers between devices with their start and end apart: 82 -> 82, of which waited for: 40 -> 39; matrix products, arithmetic and copies ran while one was open for 7% -> 7% of each run, Pallas kernels for 10% -> 10%
where the time goes in v1:
time: 468 us; the launch traced here: 459 us
  waiting for transfers between devices  178 us (38%)
  starting transfers between devices  125 us (27%)
  Pallas kernels  99.1 us (21%)
  other arithmetic  28.5 us (6%)
  local copies, waits for them, and re-layouts  22.6 us (5%)
  between operations  4.8 us (1%)
    ppermute x65, waiting for transfers between devices, swap(): return lax.ppermute(values, axis, [(i, i ^ bit) for i in range(count)])  117 us
    ppermute x65, starting transfers between devices, swap(): return lax.ppermute(values, axis, [(i, i ^ bit) for i in range(count)])  101 us
    ppermute x2, waiting for transfers between devices, hop(): first = lax.ppermute(rows[0], 'section', [(source, 1 - source)])  40.7 us
    pallas_call x2, Pallas kernels, attn_bwd(): pl.pallas_call(attn_bwd_kernel, in_specs=[smem()] * 2 + [vmem()] * 5 + [h...  31.5 us
    pallas_call x2, Pallas kernels, ffn_bwd(): pl.pallas_call(ffn_bwd_kernel, in_specs=[smem(), vmem()] + [hbm()] * (7 +...  18.3 us
    pallas_call x2, Pallas kernels, attn_fwd(): pl.pallas_call(attn_fwd_kernel, in_specs=[smem()] * 2 + [vmem()] * 3 + [h...  17.6 us
    convert_element_type x10, other arithmetic, total_of(): functools.reduce(jnp.add, [part(array, picks + more) for array, picks in...  15.5 us
    ppermute x9, starting transfers between devices, swap_cores(): return lax.ppermute(values, ('dp', 'mp'), perm)  14 us
  transfers between devices with their start and end apart: 82, of which 39 were waited for; matrix products, arithmetic and copies ran while one was open for 7% of the time, Pallas kernels for 10%

profile of v1, /device:TPU:8, one launch (start us, length us, event | category | flops | bytes accessed | tf_op | source)
XLA Modules:
  0.0 458.7 jit_solution(15225102260942597427)
XLA Ops:
  10.1 7.2 %collective-permute-done.2 = f32[32,3]{0,1:T(4,128)S(1)} collective-permute-done((f32[32,3]{0,1:T(4,128)S(1)}, f32[32,3]{0,1:T(4,128)S(1)}, u32[]{:S(2)}, u32[]{:S(2)}) %collective-permute-start.2) | collective-permute-done | bytes 416 | tf_op jit(solution)/shard_map/ppermute | solution.py:937
  27.8 10.1 %collective-permute-start.19 = (bf16[192,768]{1,0:T(8,128)(2,1)S(1)}, bf16[192,768]{1,0:T(8,128)(2,1)S(1)}, u32[]{:S(2)}, u32[]{:S(2)}) collective-permute-start(bf16[192,768]{1,0:T(8,128)(2,1)S(1)} %copy-done.33), channel_id=1, source_target_pairs={{0,4},{4,0},{8,12},{12,8},{1,5},{5,1},{9,13},{13,9},{2,6},{6,2},{1... | collective-permute-start | bytes 884744 | tf_op jit(solution)/shard_map/ppermute | solution.py:937
  37.9 3.9 collective-permute-start.21
  43.5 3.4 collective-permute-start.12
  47.2 4.6 %collective-permute-done.10.refs_10_ = bf16[192,768]{1,0:T(8,128)(2,1)S(1)} collective-permute-done((bf16[192,768]{1,0:T(8,128)(2,1)}, bf16[192,768]{1,0:T(8,128)(2,1)S(1)}, u32[]{:S(2)}, u32[]{:S(2)}) %collective-permute-start.10) | collective-permute-done | bytes 294944 | tf_op jit(solution)/shard_map/ppermute | solution.py:937
  51.8 3.4 collective-permute-done.11.refs_1_
  70.9 16.2 %attn_fwd.2 = (bf16[512,768]{1,0:T(8,128)(2,1)}, bf16[4,512,576]{2,1,0:T(8,128)(2,1)}, f32[4,8,512]{2,1,0:T(8,128)}, bf16[4,512,192]{2,1,0:T(8,128)(2,1)}, f32[512,768]{1,0:T(8,128)}, /*index=5*/bf16[512,768]{1,0:T(8,128)(2,1)}) custom-call(s32[5]{0:T(128)} %stack.91.flags, f32[32,12]{1,0:T(8,128)} %copy.67.table.table_ref, f32[32,12]{1,0:T(8,128)} %copy.67.table.table_ref, ...), custom_call_target="tpu_custom_call" | custom-call | flops 14000000000 | bytes 16777216 | tf_op jit(solution)/shard_map/attn_fwd/pallas_call | solution.py:704
  100.1 7.3 %collective-permute-done.29.refs_15_ = bf16[192,768]{1,0:T(8,128)(2,1)S(1)} collective-permute-done((bf16[192,768]{1,0:T(8,128)(2,1)S(1)}, bf16[192,768]{1,0:T(8,128)(2,1)S(1)}, u32[]{:S(2)}, u32[]{:S(2)}) %collective-permute-start.29) | collective-permute-done | bytes 294944 | tf_op jit(solution)/shard_map/ppermute | solution.py:937
  107.3 5.6 %collective-permute-done.31.refs_10_ = bf16[192,768]{1,0:T(8,128)(2,1)S(1)} collective-permute-done((bf16[192,768]{1,0:T(8,128)(2,1)S(1)}, bf16[192,768]{1,0:T(8,128)(2,1)S(1)}, u32[]{:S(2)}, u32[]{:S(2)}) %collective-permute-start.31) | collective-permute-done | bytes 294944 | tf_op jit(solution)/shard_map/ppermute | solution.py:937
  114.7 6.7 %collective-permute-done.42.refs_23_ = bf16[192,768]{1,0:T(8,128)(2,1)S(1)} collective-permute-done((bf16[192,768]{1,0:T(8,128)(2,1)}, bf16[192,768]{1,0:T(8,128)(2,1)S(1)}, u32[]{:S(2)}, u32[]{:S(2)}) %collective-permute-start.42) | collective-permute-done | bytes 294944 | tf_op jit(solution)/shard_map/ppermute | solution.py:937
  126.4 11.4 %ffn_fwd.2 = (f32[512,768]{1,0:T(8,128)}, bf16[256,768]{1,0:T(8,128)(2,1)}, bf16[256,768]{1,0:T(8,128)(2,1)}, bf16[4,512,512]{2,1,0:T(8,128)(2,1)}, bf16[4,512,5...) custom-call(s32[5]{0:T(128)} %stack.91.flags, ...), custom_call_target="tpu_custom_call" | custom-call | flops 10000000000 | bytes 16777216 | tf_op jit(solution)/shard_map/ffn_fwd/pallas_call | solution.py:726
  141.1 5.1 %collective-permute-done.45.x_low = bf16[256,768]{1,0:T(8,128)(2,1)S(1)} collective-permute-done((bf16[256,768]{1,0:T(8,128)(2,1)}, bf16[256,768]{1,0:T(8,128)(2,1)S(1)}, u32[]{:S(2)}, u32[]{:S(2)}) %collective-permute-start.45) | collective-permute-done | bytes 393248 | tf_op jit(solution)/shard_map/ppermute | solution.py:951
  146.2 4.2 collective-permute-done.46.x_high
  157.5 10.7 %collective-permute-start.50 = (bf16[8,256,128]{2,1,0:T(8,128)(2,1)S(1)}, bf16[8,256,128]{2,1,0:T(8,128)(2,1)S(1)}, u32[]{:S(2)}, u32[]{:S(2)}) collective-permute-start(bf16[8,256,128]{2,1,0:T(8,128)(2,1)S(1)} %pad_maximum_fusion.3), channel_id=1, source_target_pairs={{0,4},{4,0},{8,12},{12,8},{1,5},{5,1},{9,13},{13,9},{2,6},{6,2},{1... | collective-permute-start | bytes 1572872 | tf_op jit(solution)/shard_map/ppermute | solution.py:937
  170.4 4.2 score.1
  175.6 3.9 collective-permute-start.51
  182.4 3.5 collective-permute-start.52
  203.0 3.5 head_bwd.1
  206.5 26.7 %collective-permute-start.58 = (bf16[144,768]{1,0:T(8,128)(2,1)}, bf16[144,768]{1,0:T(8,128)(2,1)S(1)}, u32[]{:S(2)}, u32[]{:S(2)}) collective-permute-start(bf16[144,768]{1,0:T(8,128)(2,1)} %get-tuple-element.245), channel_id=1, source_target_pairs={{0,16},{16,0},{1,17},{17,1},{2,18},{18,2},{3,19},{19,3},{4,20},{20... | collective-permute-start | bytes 663560 | tf_op jit(solution)/shard_map/ppermute | solution.py:937
  238.2 7.2 %attn_bwd.2 = (bf16[256,768]{1,0:T(8,128)(2,1)}, bf16[256,768]{1,0:T(8,128)(2,1)}, f32[1,768]{1,0:T(1,128)}, bf16[4,2,208,768]{3,2,1,0:T(8,128)(2,1)}, bf16[4,2,208,768]{3,2,1,0:T(8,128)(2,1)}) custom-call(s32[5]{0:T(128)} %stack.94.flags, f32[32,12]{1,0:T(8,128)} %copy.67.table.table_ref, f32[32,12]{1,0:T(8,128)} %copy.67.table.table_ref, ...), custom_call_target="tpu_custom_call" | custom-call | flops 24999999488 | bytes 16777216 | tf_op jit(solution)/shard_map/attn_bwd/pallas_call | solution.py:906
  248.0 35.6 %collective-permute-done.59.gout_low = bf16[256,768]{1,0:T(8,128)(2,1)S(1)} collective-permute-done((bf16[256,768]{1,0:T(8,128)(2,1)}, bf16[256,768]{1,0:T(8,128)(2,1)S(1)}, u32[]{:S(2)}, u32[]{:S(2)}) %collective-permute-start.59) | collective-permute-done | bytes 393248 | tf_op jit(solution)/shard_map/ppermute | solution.py:951
  283.6 7.4 %collective-permute-done.60.gout_high = bf16[256,768]{1,0:T(8,128)(2,1)S(1)} collective-permute-done((bf16[256,768]{1,0:T(8,128)(2,1)}, bf16[256,768]{1,0:T(8,128)(2,1)S(1)}, u32[]{:S(2)}, u32[]{:S(2)}) %collective-permute-start.60) | collective-permute-done | bytes 393248 | tf_op jit(solution)/shard_map/ppermute | solution.py:954
  291.8 16.9 %ffn_bwd.3 = (f32[512,768]{1,0:T(8,128)}, f32[1,768]{1,0:T(1,128)}, bf16[4,384,768]{2,1,0:T(8,128)(2,1)}, bf16[4,384,768]{2,1,0:T(8,128)(2,1)}, bf16[4,384,768]{...) custom-call(s32[5]{0:T(128)} %stack.91.flags, ...), custom_call_target="tpu_custom_call", output_to_operand_aliasing={{1}: (35, {}), {2}: (36, {}), {3}: (37, {}), {4}: (38, {}),... | custom-call | flops 20000000000 | bytes 16777216 | tf_op jit(solution)/shard_map/ffn_bwd/pallas_call | solution.py:876
  309.3 6.8 %collective-permute-done.61 = bf16[4,384,768]{2,1,0:T(8,128)(2,1)S(1)} collective-permute-done((bf16[4,384,768]{2,1,0:T(8,128)(2,1)}, bf16[4,384,768]{2,1,0:T(8,128)(2,1)S(1)}, u32[]{:S(2)}, u32[]{:S(2)}) %collective-permute-start.61) | collective-permute-done | bytes 2359328 | tf_op jit(solution)/shard_map/ppermute | solution.py:937
  322.4 24.3 %attn_bwd.3 = (bf16[256,768]{1,0:T(8,128)(2,1)}, bf16[256,768]{1,0:T(8,128)(2,1)}, f32[1,768]{1,0:T(1,128)}, bf16[4,2,208,768]{3,2,1,0:T(8,128)(2,1)}, bf16[4,2,208,768]{3,2,1,0:T(8,128)(2,1)}) custom-call(s32[5]{0:T(128)} %stack.91.flags, ...), custom_call_target="tpu_custom_call", output_to_operand_aliasing={{0}: (27, {}), {1}: (28, {}), {2}: (29, {}), {3}: (30, {}),... | custom-call | flops 24999999488 | bytes 16777216 | tf_op jit(solution)/shard_map/attn_bwd/pallas_call | solution.py:906
  359.4 23.0 %collective-permute-done.66 = bf16[2,192,768]{2,1,0:T(8,128)(2,1)} collective-permute-done((bf16[2,192,768]{2,1,0:T(8,128)(2,1)}, bf16[2,192,768]{2,1,0:T(8,128)(2,1)}, u32[]{:S(2)}, u32[]{:S(2)}) %collective-permute-start.66) | collective-permute-done | bytes 589856 | tf_op jit(solution)/shard_map/ppermute | solution.py:937
  394.7 15.5 %collective-permute-done.76 = bf16[192,768]{1,0:T(8,128)(2,1)S(1)} collective-permute-done((bf16[192,768]{1,0:T(8,128)(2,1)S(1)}, bf16[192,768]{1,0:T(8,128)(2,1)S(1)}, u32[]{:S(2)}, u32[]{:S(2)}) %collective-permute-start.76) | collective-permute-done | bytes 294944 | tf_op jit(solution)/shard_map/ppermute | solution.py:937
  414.2 4.7 %collective-permute-done.77 = bf16[192,768]{1,0:T(8,128)(2,1)S(1)} collective-permute-done((bf16[192,768]{1,0:T(8,128)(2,1)S(1)}, bf16[192,768]{1,0:T(8,128)(2,1)S(1)}, u32[]{:S(2)}, u32[]{:S(2)}) %collective-permute-start.77) | collective-permute-done | bytes 294944 | tf_op jit(solution)/shard_map/ppermute | solution.py:937
  419.8 6.3 %collective-permute-done.70 = bf16[208,768]{1,0:T(8,128)(2,1)S(1)} collective-permute-done((bf16[208,768]{1,0:T(8,128)(2,1)S(1)}, bf16[208,768]{1,0:T(8,128)(2,1)S(1)}, u32[]{:S(2)}, u32[]{:S(2)}) %collective-permute-start.70) | collective-permute-done | bytes 319520 | tf_op jit(solution)/shard_map/ppermute | solution.py:937
  428.2 3.7 collective-permute-start.74
  433.8 4.3 finish.3
  442.0 5.8 %collective-permute-start.75 = (bf16[2,208,768]{2,1,0:T(8,128)(2,1)S(1)}, bf16[2,208,768]{2,1,0:T(8,128)(2,1)S(1)}, u32[]{:S(2)}, u32[]{:S(2)}) collective-permute-start(bf16[2,208,768]{2,1,0:T(8,128)(2,1)S(1)} %maximum_select_fusion.1.mine), channel_id=1, source_target_pairs={{0,4},{4,0},{8,12},{12,8},{1,5},{5,1},{9,13},{13,9},{2,6},{6,2},{1... | collective-permute-start | bytes 1916936 | tf_op jit(solution)/shard_map/ppermute | solution.py:937
  (391 shorter events, 150.7 us)
Async XLA Ops:
  2.1 16.5 %collective-permute-start = (bf16[192,768]{1,0:T(8,128)(2,1)S(1)}, bf16[192,768]{1,0:T(8,128)(2,1)S(1)}, u32[]{:S(2)}, u32[]{:S(2)}) collective-permute-start(bf16[192,768]{1,0:T(8,128)(2,1)S(1)} %constant_dynamic-slice_fusion), channel_id=1, source_target_pairs={{0,1},{1,0},{2,3},{3,2},{4,5},{5,4},{6,7},{7,6},{8,9},{9,8},{10,11... | collective-permute-start | bytes 884744 | tf_op jit(solution)/shard_map/ppermute | solution.py:937
  2.1 16.5 %collective-permute-start.1 = (bf16[192,768]{1,0:T(8,128)(2,1)S(1)}, bf16[192,768]{1,0:T(8,128)(2,1)}, u32[]{:S(2)}, u32[]{:S(2)}) collective-permute-start(bf16[192,768]{1,0:T(8,128)(2,1)S(1)} %constant_dynamic-slice_fusion), channel_id=1, source_target_pairs={{0,2},{1,3},{2,0},{3,1},{4,6},{5,7},{6,4},{7,5},{8,10},{9,11},{10,... | collective-permute-start | bytes 884744 | tf_op jit(solution)/shard_map/ppermute | solution.py:937
  18.6 23.2 %collective-permute-start.5 = (bf16[192,768]{1,0:T(8,128)(2,1)}, bf16[192,768]{1,0:T(8,128)(2,1)}, u32[]{:S(2)}, u32[]{:S(2)}) collective-permute-start(bf16[192,768]{1,0:T(8,128)(2,1)} %collective-permute-done.1.refs_5_), channel_id=1, source_target_pairs={{0,1},{1,0},{2,3},{3,2},{4,5},{5,4},{6,7},{7,6},{8,9},{9,8},{10,11... | collective-permute-start | bytes 884744 | tf_op jit(solution)/shard_map/ppermute | solution.py:937
  20.2 21.6 %collective-permute-start.7 = (bf16[192,768]{1,0:T(8,128)(2,1)}, bf16[192,768]{1,0:T(8,128)(2,1)}, u32[]{:S(2)}, u32[]{:S(2)}) collective-permute-start(bf16[192,768]{1,0:T(8,128)(2,1)} %collective-permute-done.1.refs_5_), channel_id=1, source_target_pairs={{0,8},{4,12},{8,0},{12,4},{1,9},{5,13},{9,1},{13,5},{2,10},{6,14},... | collective-permute-start | bytes 884744 | tf_op jit(solution)/shard_map/ppermute | solution.py:937
  25.0 12.9 %collective-permute-start.9 = (bf16[192,768]{1,0:T(8,128)(2,1)S(1)}, bf16[192,768]{1,0:T(8,128)(2,1)S(1)}, u32[]{:S(2)}, u32[]{:S(2)}) collective-permute-start(bf16[192,768]{1,0:T(8,128)(2,1)S(1)} %get-tuple-element.330), channel_id=1, source_target_pairs={{0,1},{1,0},{2,5},{3,4},{4,3},{5,2},{6,7},{7,6},{8,9},{9,8},{10,13... | collective-permute-start | bytes 884744 | tf_op jit(solution)/shard_map/ppermute | solution.py:1015
  25.6 16.2 %collective-permute-start.6 = (bf16[192,768]{1,0:T(8,128)(2,1)}, bf16[192,768]{1,0:T(8,128)(2,1)S(1)}, u32[]{:S(2)}, u32[]{:S(2)}) collective-permute-start(bf16[192,768]{1,0:T(8,128)(2,1)} %copy-done.32), channel_id=1, source_target_pairs={{0,8},{4,12},{8,0},{12,4},{1,9},{5,13},{9,1},{13,5},{2,10},{6,14},... | collective-permute-start | bytes 884744 | tf_op jit(solution)/shard_map/ppermute | solution.py:937
  27.8 32.4 %collective-permute-start.19 = (bf16[192,768]{1,0:T(8,128)(2,1)S(1)}, bf16[192,768]{1,0:T(8,128)(2,1)S(1)}, u32[]{:S(2)}, u32[]{:S(2)}) collective-permute-start(bf16[192,768]{1,0:T(8,128)(2,1)S(1)} %copy-done.33), channel_id=1, source_target_pairs={{0,4},{4,0},{8,12},{12,8},{1,5},{5,1},{9,13},{13,9},{2,6},{6,2},{1... | collective-permute-start | bytes 884744 | tf_op jit(solution)/shard_map/ppermute | solution.py:937
  37.9 22.4 %collective-permute-start.21 = (bf16[192,768]{1,0:T(8,128)(2,1)}, bf16[192,768]{1,0:T(8,128)(2,1)S(1)}, u32[]{:S(2)}, u32[]{:S(2)}) collective-permute-start(bf16[192,768]{1,0:T(8,128)(2,1)} %collective-permute-done.1.refs_5_), channel_id=1, source_target_pairs={{0,4},{4,0},{8,12},{12,8},{1,5},{5,1},{9,13},{13,9},{2,6},{6,2},{1... | collective-permute-start | bytes 884744 | tf_op jit(solution)/shard_map/ppermute | solution.py:937
  43.5 15.8 %collective-permute-start.12 = (bf16[192,768]{1,0:T(8,128)(2,1)S(1)}, bf16[192,768]{1,0:T(8,128)(2,1)S(1)}, u32[]{:S(2)}, u32[]{:S(2)}) collective-permute-start(bf16[192,768]{1,0:T(8,128)(2,1)S(1)} %get-tuple-element.180), channel_id=1, source_target_pairs={{0,2},{1,3},{2,0},{3,1},{4,6},{5,7},{6,4},{7,5},{8,10},{9,11},{10,... | collective-permute-start | bytes 884744 | tf_op jit(solution)/shard_map/ppermute | solution.py:937
  63.1 24.1 %collective-permute-start.14 = (bf16[192,768]{1,0:T(8,128)(2,1)}, bf16[192,768]{1,0:T(8,128)(2,1)S(1)}, u32[]{:S(2)}, u32[]{:S(2)}) collective-permute-start(bf16[192,768]{1,0:T(8,128)(2,1)} %copy-done.40), channel_id=1, source_target_pairs={{0,1},{1,0},{2,3},{3,2},{4,5},{5,4},{6,7},{7,6},{8,9},{9,8},{10,11... | collective-permute-start | bytes 884744 | tf_op jit(solution)/shard_map/ppermute | solution.py:937
  65.3 22.0 %collective-permute-start.16 = (bf16[192,768]{1,0:T(8,128)(2,1)}, bf16[192,768]{1,0:T(8,128)(2,1)S(1)}, u32[]{:S(2)}, u32[]{:S(2)}) collective-permute-start(bf16[192,768]{1,0:T(8,128)(2,1)} %copy-done.40), channel_id=1, source_target_pairs={{0,8},{4,12},{8,0},{12,4},{1,9},{5,13},{9,1},{13,5},{2,10},{6,14},... | collective-permute-start | bytes 884744 | tf_op jit(solution)/shard_map/ppermute | solution.py:937
  66.7 20.5 %collective-permute-start.17 = (bf16[192,768]{1,0:T(8,128)(2,1)S(1)}, bf16[192,768]{1,0:T(8,128)(2,1)S(1)}, u32[]{:S(2)}, u32[]{:S(2)}) collective-permute-start(bf16[192,768]{1,0:T(8,128)(2,1)S(1)} %get-tuple-element.193), channel_id=1, source_target_pairs={{0,1},{1,0},{2,3},{3,2},{4,5},{5,4},{6,7},{7,6},{8,9},{9,8},{10,11... | collective-permute-start | bytes 884744 | tf_op jit(solution)/shard_map/ppermute | solution.py:937
  67.4 19.9 %collective-permute-start.18 = (bf16[192,768]{1,0:T(8,128)(2,1)S(1)}, bf16[192,768]{1,0:T(8,128)(2,1)S(1)}, u32[]{:S(2)}, u32[]{:S(2)}) collective-permute-start(bf16[192,768]{1,0:T(8,128)(2,1)S(1)} %get-tuple-element.193), channel_id=1, source_target_pairs={{0,2},{1,3},{2,0},{3,1},{4,6},{5,7},{6,4},{7,5},{8,10},{9,11},{10,... | collective-permute-start | bytes 884744 | tf_op jit(solution)/shard_map/ppermute | solution.py:937
  70.2 17.0 %collective-permute-start.15 = (bf16[192,768]{1,0:T(8,128)(2,1)}, bf16[192,768]{1,0:T(8,128)(2,1)S(1)}, u32[]{:S(2)}, u32[]{:S(2)}) collective-permute-start(bf16[192,768]{1,0:T(8,128)(2,1)} %collective-permute-done.11.refs_1_), channel_id=1, source_target_pairs={{0,8},{4,12},{8,0},{12,4},{1,9},{5,13},{9,1},{13,5},{2,10},{6,14},... | collective-permute-start | bytes 884744 | tf_op jit(solution)/shard_map/ppermute | solution.py:937
  87.2 26.9 %collective-permute-start.32 = (bf16[192,768]{1,0:T(8,128)(2,1)}, bf16[192,768]{1,0:T(8,128)(2,1)S(1)}, u32[]{:S(2)}, u32[]{:S(2)}) collective-permute-start(bf16[192,768]{1,0:T(8,128)(2,1)} %collective-permute-done.11.refs_1_), channel_id=1, source_target_pairs={{0,4},{4,0},{8,12},{12,8},{1,5},{5,1},{9,13},{13,9},{2,6},{6,2},{1... | collective-permute-start | bytes 884744 | tf_op jit(solution)/shard_map/ppermute | solution.py:937
  90.9 16.4 %collective-permute-start.30 = (bf16[192,768]{1,0:T(8,128)(2,1)}, bf16[192,768]{1,0:T(8,128)(2,1)}, u32[]{:S(2)}, u32[]{:S(2)}) collective-permute-start(bf16[192,768]{1,0:T(8,128)(2,1)} %copy-done.47), channel_id=1, source_target_pairs={{0,8},{4,12},{8,0},{12,4},{1,9},{5,13},{9,1},{13,5},{2,10},{6,14},... | collective-permute-start | bytes 884744 | tf_op jit(solution)/shard_map/ppermute | solution.py:937
  97.1 15.8 %collective-permute-start.31 = (bf16[192,768]{1,0:T(8,128)(2,1)S(1)}, bf16[192,768]{1,0:T(8,128)(2,1)S(1)}, u32[]{:S(2)}, u32[]{:S(2)}) collective-permute-start(bf16[192,768]{1,0:T(8,128)(2,1)S(1)} %collective-permute-done.14.refs_9_), channel_id=1, source_target_pairs={{0,8},{4,12},{8,0},{12,4},{1,9},{5,13},{9,1},{13,5},{2,10},{6,14},... | collective-permute-start | bytes 884744 | tf_op jit(solution)/shard_map/ppermute | solution.py:937
  100.1 14.2 %collective-permute-start.34 = (bf16[192,768]{1,0:T(8,128)(2,1)S(1)}, bf16[192,768]{1,0:T(8,128)(2,1)S(1)}, u32[]{:S(2)}, u32[]{:S(2)}) collective-permute-start(bf16[192,768]{1,0:T(8,128)(2,1)S(1)} %copy-done.41), channel_id=1, source_target_pairs={{0,4},{4,0},{8,12},{12,8},{1,5},{5,1},{9,13},{13,9},{2,6},{6,2},{1... | collective-permute-start | bytes 884744 | tf_op jit(solution)/shard_map/ppermute | solution.py:937
  206.5 30.8 %collective-permute-start.58 = (bf16[144,768]{1,0:T(8,128)(2,1)}, bf16[144,768]{1,0:T(8,128)(2,1)S(1)}, u32[]{:S(2)}, u32[]{:S(2)}) collective-permute-start(bf16[144,768]{1,0:T(8,128)(2,1)} %get-tuple-element.245), channel_id=1, source_target_pairs={{0,16},{16,0},{1,17},{17,1},{2,18},{18,2},{3,19},{19,3},{4,20},{20... | collective-permute-start | bytes 663560 | tf_op jit(solution)/shard_map/ppermute | solution.py:937
  245.4 38.2 %collective-permute-start.59 = (bf16[256,768]{1,0:T(8,128)(2,1)}, bf16[256,768]{1,0:T(8,128)(2,1)S(1)}, u32[]{:S(2)}, u32[]{:S(2)}) collective-permute-start(bf16[256,768]{1,0:T(8,128)(2,1)} %get-tuple-element.251.refs_13_), channel_id=1, source_target_pairs={{16,0},{17,1},{18,2},{19,3},{20,4},{21,5},{22,6},{23,7},{24,8},{25... | collective-permute-start | bytes 1179656 | tf_op jit(solution)/shard_map/ppermute | solution.py:951
  246.7 44.2 %collective-permute-start.60 = (bf16[256,768]{1,0:T(8,128)(2,1)}, bf16[256,768]{1,0:T(8,128)(2,1)S(1)}, u32[]{:S(2)}, u32[]{:S(2)}) collective-permute-start(bf16[256,768]{1,0:T(8,128)(2,1)} %get-tuple-element.252.refs_14_), channel_id=1, source_target_pairs={{16,0},{24,8},{17,1},{25,9},{18,2},{26,10},{19,3},{27,11}} | collective-permute-start | bytes 1179656 | tf_op jit(solution)/shard_map/ppermute | solution.py:954
  319.1 28.4 %collective-permute-start.64 = (bf16[2,2,192,768]{3,2,1,0:T(8,128)(2,1)S(1)}, bf16[2,2,192,768]{3,2,1,0:T(8,128)(2,1)S(1)}, u32[]{:S(2)}, u32[]{:S(2)}) collective-permute-start(bf16[2,2,192,768]{3,2,1,0:T(8,128)(2,1)S(1)} %fusion.3), channel_id=1, source_target_pairs={{0,1},{1,0},{2,3},{3,2},{4,5},{5,4},{6,7},{7,6},{8,9},{9,8},{10,11... | collective-permute-start | bytes 3538952 | tf_op jit(solution)/shard_map/ppermute | solution.py:937
  321.5 27.8 %collective-permute-start.63 = (bf16[2,2,192,768]{3,2,1,0:T(8,128)(2,1)S(1)}, bf16[2,2,192,768]{3,2,1,0:T(8,128)(2,1)S(1)}, u32[]{:S(2)}, u32[]{:S(2)}) collective-permute-start(bf16[2,2,192,768]{3,2,1,0:T(8,128)(2,1)S(1)} %fusion.2), channel_id=1, source_target_pairs={{0,8},{4,12},{8,0},{12,4},{1,9},{5,13},{9,1},{13,5},{2,10},{6,14},... | collective-permute-start | bytes 3538952 | tf_op jit(solution)/shard_map/ppermute | solution.py:937
  356.7 30.4 %collective-permute-start.68 = (bf16[2,2,208,768]{3,2,1,0:T(8,128)(2,1)}, bf16[2,2,208,768]{3,2,1,0:T(8,128)(2,1)}, u32[]{:S(2)}, u32[]{:S(2)}) collective-permute-start(bf16[2,2,208,768]{3,2,1,0:T(8,128)(2,1)} %fusion), channel_id=1, source_target_pairs={{0,8},{4,12},{8,0},{12,4},{1,9},{5,13},{9,1},{13,5},{2,10},{6,14},... | collective-permute-start | bytes 3833864 | tf_op jit(solution)/shard_map/ppermute | solution.py:937
  357.5 25.0 %collective-permute-start.66 = (bf16[2,192,768]{2,1,0:T(8,128)(2,1)}, bf16[2,192,768]{2,1,0:T(8,128)(2,1)}, u32[]{:S(2)}, u32[]{:S(2)}) collective-permute-start(bf16[2,192,768]{2,1,0:T(8,128)(2,1)} %get-tuple-element.291), channel_id=1, source_target_pairs={{0,1},{1,0},{2,3},{3,2},{4,5},{5,4},{6,7},{7,6},{8,9},{9,8},{10,11... | collective-permute-start | bytes 1769480 | tf_op jit(solution)/shard_map/ppermute | solution.py:937
  358.1 27.4 %collective-permute-start.67 = (bf16[2,192,768]{2,1,0:T(8,128)(2,1)S(1)}, bf16[2,192,768]{2,1,0:T(8,128)(2,1)}, u32[]{:S(2)}, u32[]{:S(2)}) collective-permute-start(bf16[2,192,768]{2,1,0:T(8,128)(2,1)S(1)} %get-tuple-element.292), channel_id=1, source_target_pairs={{0,2},{1,3},{2,0},{3,1},{4,6},{5,7},{6,4},{7,5},{8,10},{9,11},{10,... | collective-permute-start | bytes 1769480 | tf_op jit(solution)/shard_map/ppermute | solution.py:937
  359.4 35.2 %collective-permute-start.71 = (bf16[128,768]{1,0:T(8,128)(2,1)S(1)}, bf16[128,768]{1,0:T(8,128)(2,1)S(1)}, u32[]{:S(2)}, u32[]{:S(2)}) collective-permute-start(bf16[128,768]{1,0:T(8,128)(2,1)S(1)} %slice.129), channel_id=1, source_target_pairs={{0,4},{4,0},{8,12},{12,8},{1,5},{5,1},{9,13},{13,9},{2,6},{6,2},{1... | collective-permute-start | bytes 589832 | tf_op jit(solution)/shard_map/ppermute | solution.py:937
  388.7 24.0 %collective-permute-start.69 = (bf16[2,208,768]{2,1,0:T(8,128)(2,1)S(1)}, bf16[2,208,768]{2,1,0:T(8,128)(2,1)S(1)}, u32[]{:S(2)}, u32[]{:S(2)}) collective-permute-start(bf16[2,208,768]{2,1,0:T(8,128)(2,1)S(1)} %fusion.1), channel_id=1, source_target_pairs={{0,1},{1,0},{2,3},{3,2},{4,5},{5,4},{6,7},{7,6},{8,9},{9,8},{10,11... | collective-permute-start | bytes 1916936 | tf_op jit(solution)/shard_map/ppermute | solution.py:937
  390.9 19.3 %collective-permute-start.76 = (bf16[192,768]{1,0:T(8,128)(2,1)S(1)}, bf16[192,768]{1,0:T(8,128)(2,1)S(1)}, u32[]{:S(2)}, u32[]{:S(2)}) collective-permute-start(bf16[192,768]{1,0:T(8,128)(2,1)S(1)} %fusion.11), channel_id=1, source_target_pairs={{0,2},{1,3},{2,0},{3,1},{4,6},{5,7},{6,4},{7,5},{8,10},{9,11},{10,... | collective-permute-start | bytes 884744 | tf_op jit(solution)/shard_map/ppermute | solution.py:937
  393.4 20.5 %collective-permute-start.79 = (bf16[2,192,768]{2,1,0:T(8,128)(2,1)S(1)}, bf16[2,192,768]{2,1,0:T(8,128)(2,1)S(1)}, u32[]{:S(2)}, u32[]{:S(2)}) collective-permute-start(bf16[2,192,768]{2,1,0:T(8,128)(2,1)S(1)} %fusion.5), channel_id=1, source_target_pairs={{0,8},{4,12},{8,0},{12,4},{1,9},{5,13},{9,1},{13,5},{2,10},{6,14},... | collective-permute-start | bytes 1769480 | tf_op jit(solution)/shard_map/ppermute | solution.py:937
  414.1 19.6 %collective-permute-start.80 = (bf16[2,192,768]{2,1,0:T(8,128)(2,1)S(1)}, bf16[2,192,768]{2,1,0:T(8,128)(2,1)}, u32[]{:S(2)}, u32[]{:S(2)}) collective-permute-start(bf16[2,192,768]{2,1,0:T(8,128)(2,1)S(1)} %add_convert_fusion.3.mine2), channel_id=1, source_target_pairs={{0,4},{4,0},{8,12},{12,8},{1,5},{5,1},{9,13},{13,9},{2,6},{6,2},{1... | collective-permute-start | bytes 1769480 | tf_op jit(solution)/shard_map/ppermute | solution.py:937
  419.8 13.9 %collective-permute-start.78 = (bf16[2,192,768]{2,1,0:T(8,128)(2,1)}, bf16[2,192,768]{2,1,0:T(8,128)(2,1)}, u32[]{:S(2)}, u32[]{:S(2)}) collective-permute-start(bf16[2,192,768]{2,1,0:T(8,128)(2,1)} %maximum_select_fusion.4.mine1), channel_id=1, source_target_pairs={{0,4},{4,0},{8,12},{12,8},{1,5},{5,1},{9,13},{13,9},{2,6},{6,2},{1... | collective-permute-start | bytes 1769480 | tf_op jit(solution)/shard_map/ppermute | solution.py:937
  (117 other events, 886.6 us)
